TPU v7x, 512 devices: a whole 4x4x16 slice. The times are simulated.
512 devices in a mesh: stream: 16 (over z), pitch: 32 (over y, x, core).
Axes of the slice: x: 4, y: 4, z: 16, core: 2. Of those that a mesh axis runs over, the one named last changes fastest.
Arguments:
- flow_state: float32 [5, 256, 16384], P(None, 'stream', 'pitch'), may hold values from -6 to 6
- residual: float32 [5, 256, 16384], P(None, 'stream', 'pitch'), may hold values from -3 to 3
- spread: float32 [256, 16384], P('stream', 'pitch'), may hold values from 0.02 to 0.2
- diag_inv: float32 [25, 256, 16384], P(None, 'stream', 'pitch'), may hold values from -0.2 to 1, as said below
- lower_jac: float32 [25, 256, 16384], P(None, 'stream', 'pitch'), may hold values from -0.2 to 1.5, as said below
- upper_jac: float32 [25, 256, 16384], P(None, 'stream', 'pitch'), may hold values from -0.2 to 1.5, as said below
- partner: int32 [128], replicated, may hold values from 0 to 127, as said below
Outputs:
- updated: float32 [5, 256, 16384], P(None, 'stream', 'pitch')
Inputs may be any that keep to these rules, and one draw needn't show every extreme that they name: `partner`: a permutation of the pitch positions. `diag_inv`: each cell's block has a positive diagonal. `lower_jac`: each cell's block has a positive diagonal. `upper_jac`: each cell's block has a positive diagonal.
All inputs are finite; a program needn't handle non-finite values.
Results may differ from a plain program's by a relative error of at most 0.00012.
Values sent between devices are 32-bit elements; how exact they have to be, the bound alone decides.
A program may use at most 64 MiB of HBM per device.

v0:
```python
import jax
import jax.numpy as jnp
from jax import lax
from jax.sharding import PartitionSpec as P

SPANC = 128


def padded_2(block, sides, width):
    for axis, dim in sides:
        count = lax.axis_size(axis)
        forward = [(i, i + 1) for i in range(count - 1)]
        forward.append((count - 1, 0))
        backward = [(target, source) for source, target in forward]
        low = lax.ppermute(
            lax.slice_in_dim(block, block.shape[dim] - width, None, axis=dim), axis, forward
        )
        high = lax.ppermute(lax.slice_in_dim(block, 0, width, axis=dim), axis, backward)
        block = jnp.concatenate([low, block, high], axis=dim)
    return block


def passed_along(value, axis, steps):
    count = lax.axis_size(axis)
    first, last = (max(0, -steps), min(count, count - steps))
    return lax.ppermute(value, axis, [(source, source + steps) for source in range(first, last)])


def apply_block(matrix, vector):
    return jnp.sum(matrix * vector[None, :, :], axis=1)


def chain_blocks(left, right):
    return jnp.sum(left[:, :, None, :] * right[None, :, :, :], axis=1)


def local(flow_state, residual, spread, diag_inv, lower_jac, upper_jac, partner):
    components, plane_count, cell_count = flow_state.shape
    stream_count = lax.axis_size("stream")
    stream_at = lax.axis_index("stream")
    pitch_at = lax.axis_index("pitch")
    span_cells = SPANC
    padded = padded_2(flow_state, (("pitch", 2),), SPANC)
    source = residual + spread[None] * (
        padded[:, :, 2 * span_cells :] + padded[:, :, :cell_count] - 2.0 * flow_state
    )
    local_interface = plane_count // 2
    rotor_plane = flow_state[:, local_interface - 1, :]
    rotor_cells = lax.all_gather(rotor_plane, "pitch", axis=1, tiled=True)
    per_device = cell_count // span_cells
    my_partners = lax.dynamic_slice_in_dim(partner, pitch_at * per_device, per_device)
    rotor_ghost = jnp.take(
        rotor_cells.reshape(components, -1, span_cells), my_partners, axis=1
    ).reshape(components, cell_count)
    inverse = diag_inv.reshape(components, components, plane_count, cell_count)
    lower_blocks = lower_jac.reshape(components, components, plane_count, cell_count)
    upper_blocks = upper_jac.reshape(components, components, plane_count, cell_count)
    interface_plane = plane_count * (stream_count // 2) + local_interface
    at_interface = (stream_at == stream_count // 2).astype(jnp.float32)
    source = source.at[:, local_interface, :].add(
        at_interface * apply_block(lower_blocks[:, :, local_interface, :], rotor_ghost)
    )
    global_plane = stream_at * plane_count + jnp.arange(plane_count)
    lower_keep = (global_plane != interface_plane).astype(jnp.float32)
    upper_keep = (global_plane != interface_plane - 1).astype(jnp.float32)
    identity = jnp.broadcast_to(
        jnp.eye(components, dtype=jnp.float32)[:, :, None], (components, components, cell_count)
    )
    zero_plane = jnp.zeros((components, cell_count), jnp.float32)

    def forward_map(plane, carry):
        matrix, vector = carry
        inv_now = lax.dynamic_index_in_dim(inverse, plane, 2, keepdims=False)
        low_now = lax.dynamic_index_in_dim(
            lower_blocks, plane, 2, keepdims=False
        ) * lax.dynamic_index_in_dim(lower_keep, plane, 0, keepdims=False)
        src_now = lax.dynamic_index_in_dim(source, plane, 1, keepdims=False)
        step_matrix = chain_blocks(inv_now, low_now)
        return (
            chain_blocks(step_matrix, matrix),
            apply_block(step_matrix, vector) + apply_block(inv_now, src_now),
        )

    front_matrix, front_vector = lax.fori_loop(0, plane_count, forward_map, (identity, zero_plane))

    def front_turn(turn, carry):
        sent_on, received = carry
        received = passed_along(sent_on, "stream", 1)
        return (apply_block(front_matrix, received) + front_vector, received)

    _, front_in = lax.fori_loop(0, stream_count - 1, front_turn, (front_vector, zero_plane))

    def forward_sweep(plane, carry):
        previous, stored = carry
        inv_now = lax.dynamic_index_in_dim(inverse, plane, 2, keepdims=False)
        low_now = lax.dynamic_index_in_dim(lower_blocks, plane, 2, keepdims=False)
        keep_now = lax.dynamic_index_in_dim(lower_keep, plane, 0, keepdims=False)
        src_now = lax.dynamic_index_in_dim(source, plane, 1, keepdims=False)
        current = apply_block(inv_now, src_now + apply_block(low_now, previous) * keep_now)
        return (current, lax.dynamic_update_index_in_dim(stored, current, plane, 1))

    _, stars = lax.fori_loop(0, plane_count, forward_sweep, (front_in, jnp.zeros_like(flow_state)))

    def backward_map(step_back, carry):
        matrix, vector = carry
        plane = plane_count - 1 - step_back
        inv_now = lax.dynamic_index_in_dim(inverse, plane, 2, keepdims=False)
        up_now = lax.dynamic_index_in_dim(
            upper_blocks, plane, 2, keepdims=False
        ) * lax.dynamic_index_in_dim(upper_keep, plane, 0, keepdims=False)
        star_now = lax.dynamic_index_in_dim(stars, plane, 1, keepdims=False)
        step_matrix = chain_blocks(inv_now, up_now)
        return (chain_blocks(step_matrix, matrix), apply_block(step_matrix, vector) + star_now)

    back_matrix, back_vector = lax.fori_loop(0, plane_count, backward_map, (identity, zero_plane))

    def back_turn(turn, carry):
        sent_on, received = carry
        received = passed_along(sent_on, "stream", -1)
        return (apply_block(back_matrix, received) + back_vector, received)

    _, back_in = lax.fori_loop(0, stream_count - 1, back_turn, (back_vector, zero_plane))

    def backward_sweep(step_back, carry):
        following, stored = carry
        plane = plane_count - 1 - step_back
        inv_now = lax.dynamic_index_in_dim(inverse, plane, 2, keepdims=False)
        up_now = lax.dynamic_index_in_dim(upper_blocks, plane, 2, keepdims=False)
        keep_now = lax.dynamic_index_in_dim(upper_keep, plane, 0, keepdims=False)
        star_now = lax.dynamic_index_in_dim(stars, plane, 1, keepdims=False)
        current = star_now + apply_block(inv_now, apply_block(up_now, following) * keep_now)
        return (current, lax.dynamic_update_index_in_dim(stored, current, plane, 1))

    _, changes = lax.fori_loop(
        0, plane_count, backward_sweep, (back_in, jnp.zeros_like(flow_state))
    )
    return flow_state + changes


def solution(mesh):
    in_specs = (
        P(None, "stream", "pitch"),
        P(None, "stream", "pitch"),
        P("stream", "pitch"),
        P(None, "stream", "pitch"),
        P(None, "stream", "pitch"),
        P(None, "stream", "pitch"),
        P(),
    )
    out_specs = P(None, "stream", "pitch")
    return jax.shard_map(local, mesh=mesh, in_specs=in_specs, out_specs=out_specs, check_vma=False)
```

profile of v0, /device:TPU:224, one launch (start us, length us, event | category | flops | bytes accessed | tf_op | source)
XLA Modules:
  0.0 466.8 jit_solution(16324201169533897004)
XLA Ops:
  1.1 6.6 %collective-permute-start.2 = (f32[5,16,128]{2,0,1:T(8,128)S(1)}, f32[5,16,128]{2,0,1:T(8,128)S(1)}, u32[]{:S(2)}, u32[]{:S(2)}) collective-permute-start(f32[5,16,128]{2,0,1:T(8,128)S(1)} %get-tuple-element.850), channel_id=1, source_target_pairs={{1,0},{2,1},{3,2},{4,3},{5,4},{6,5},{7,6},{8,7},{9,8},{10,9},{11,1... | collective-permute-start | bytes 122888 | tf_op jit(solution)/shard_map/ppermute | solution.py:18
  7.7 1.9 collective-permute-start.3
  11.3 24.3 %all-gather = f32[5,1,16384]{2,1,0:T(1,128)S(1)} all-gather(f32[5,1,512]{2,1,0:T(1,128)S(1)} %slice.48), channel_id=2, replica_groups=mesh['stream'=16,'pitch'=32] {'pitch'}, dimensions={2}, use_global_device_ids=true | all-gather | bytes 337920 | tf_op jit(solution)/shard_map/all_gather | solution.py:49
  38.4 40.8 %while.95 = (s32[]{:T(128)}, f32[5,5,512]{2,1,0:T(8,128)S(1)}, f32[5,512]{1,0:T(8,128)S(1)}, f32[5,5,16,512]{3,1,0,2:T(8,128)S(1)}, f32[5,5,16,512]{3,2,1,0:T(8,...) while((s32[]{:T(128)}, f32[5,5,512]{2,1,0:T(8,128)S(1)}, ...), condition=%wide.region_6.7_spmd.clone, body=%wide.region_1.6_spmd.clone.sunk | while | flops 294403 | bytes 880771 | solution.py:84
  79.9 111.3 %while.91 = (s32[]{:T(128)}, f32[5,512]{1,0:T(8,128)S(1)}, f32[5,512]{1,0:T(8,128)}, f32[5,5,512]{2,1,0:T(8,128)S(1)}, f32[5,512]{1,0:T(8,128)S(1)}, /*index=5*/s32[]{:T(128)}) while((s32[]{:T(128)}, f32[5,512]{1,0:T(8,128)S(1)}, f32[5,512]{1,0:T(8,128)}, f32[5,5,512]{2,1,0:T(8,128)S(1)}, f32[5,512]{1,0:T(8,128)S(1)}, ...), condition=%wide.region_9.10_spmd, body=%wide.region_7.9_spmd.sunk | while | flops 25602 | bytes 184457 | solution.py:91
  79.9 5.0 %collective-permute-start = (f32[5,512]{1,0:T(8,128)S(1)}, f32[5,512]{1,0:T(8,128)S(1)}, u32[]{:S(2)}, u32[]{:S(2)}) collective-permute-start(f32[5,512]{1,0:T(8,128)S(1)} %get-tuple-element.1136), channel_id=1, source_target_pairs={{0,32},{32,64},{64,96},{96,128},{128,160},{160,192},{192,224},{224... | collective-permute-start | bytes 30728 | tf_op jit(solution)/shard_map/while/body/eval_jaxpr/ppermute | solution.py:26
  84.9 1.4 collective-permute-done
  86.9 5.4 %collective-permute-start = (f32[5,512]{1,0:T(8,128)S(1)}, f32[5,512]{1,0:T(8,128)S(1)}, u32[]{:S(2)}, u32[]{:S(2)}) collective-permute-start(f32[5,512]{1,0:T(8,128)S(1)} %get-tuple-element.1136), channel_id=1, source_target_pairs={{0,32},{32,64},{64,96},{96,128},{128,160},{160,192},{192,224},{224... | collective-permute-start | bytes 30728 | tf_op jit(solution)/shard_map/while/body/eval_jaxpr/ppermute | solution.py:26
  92.3 1.4 collective-permute-done
  94.3 5.4 %collective-permute-start = (f32[5,512]{1,0:T(8,128)S(1)}, f32[5,512]{1,0:T(8,128)S(1)}, u32[]{:S(2)}, u32[]{:S(2)}) collective-permute-start(f32[5,512]{1,0:T(8,128)S(1)} %get-tuple-element.1136), channel_id=1, source_target_pairs={{0,32},{32,64},{64,96},{96,128},{128,160},{160,192},{192,224},{224... | collective-permute-start | bytes 30728 | tf_op jit(solution)/shard_map/while/body/eval_jaxpr/ppermute | solution.py:26
  99.8 1.4 collective-permute-done
  101.8 5.4 %collective-permute-start = (f32[5,512]{1,0:T(8,128)S(1)}, f32[5,512]{1,0:T(8,128)S(1)}, u32[]{:S(2)}, u32[]{:S(2)}) collective-permute-start(f32[5,512]{1,0:T(8,128)S(1)} %get-tuple-element.1136), channel_id=1, source_target_pairs={{0,32},{32,64},{64,96},{96,128},{128,160},{160,192},{192,224},{224... | collective-permute-start | bytes 30728 | tf_op jit(solution)/shard_map/while/body/eval_jaxpr/ppermute | solution.py:26
  107.2 1.4 collective-permute-done
  109.2 5.4 %collective-permute-start = (f32[5,512]{1,0:T(8,128)S(1)}, f32[5,512]{1,0:T(8,128)S(1)}, u32[]{:S(2)}, u32[]{:S(2)}) collective-permute-start(f32[5,512]{1,0:T(8,128)S(1)} %get-tuple-element.1136), channel_id=1, source_target_pairs={{0,32},{32,64},{64,96},{96,128},{128,160},{160,192},{192,224},{224... | collective-permute-start | bytes 30728 | tf_op jit(solution)/shard_map/while/body/eval_jaxpr/ppermute | solution.py:26
  114.6 1.4 collective-permute-done
  116.7 5.4 %collective-permute-start = (f32[5,512]{1,0:T(8,128)S(1)}, f32[5,512]{1,0:T(8,128)S(1)}, u32[]{:S(2)}, u32[]{:S(2)}) collective-permute-start(f32[5,512]{1,0:T(8,128)S(1)} %get-tuple-element.1136), channel_id=1, source_target_pairs={{0,32},{32,64},{64,96},{96,128},{128,160},{160,192},{192,224},{224... | collective-permute-start | bytes 30728 | tf_op jit(solution)/shard_map/while/body/eval_jaxpr/ppermute | solution.py:26
  122.1 1.4 collective-permute-done
  124.1 5.5 %collective-permute-start = (f32[5,512]{1,0:T(8,128)S(1)}, f32[5,512]{1,0:T(8,128)S(1)}, u32[]{:S(2)}, u32[]{:S(2)}) collective-permute-start(f32[5,512]{1,0:T(8,128)S(1)} %get-tuple-element.1136), channel_id=1, source_target_pairs={{0,32},{32,64},{64,96},{96,128},{128,160},{160,192},{192,224},{224... | collective-permute-start | bytes 30728 | tf_op jit(solution)/shard_map/while/body/eval_jaxpr/ppermute | solution.py:26
  129.6 1.4 collective-permute-done
  131.6 5.4 %collective-permute-start = (f32[5,512]{1,0:T(8,128)S(1)}, f32[5,512]{1,0:T(8,128)S(1)}, u32[]{:S(2)}, u32[]{:S(2)}) collective-permute-start(f32[5,512]{1,0:T(8,128)S(1)} %get-tuple-element.1136), channel_id=1, source_target_pairs={{0,32},{32,64},{64,96},{96,128},{128,160},{160,192},{192,224},{224... | collective-permute-start | bytes 30728 | tf_op jit(solution)/shard_map/while/body/eval_jaxpr/ppermute | solution.py:26
  137.0 1.4 collective-permute-done
  139.1 5.4 %collective-permute-start = (f32[5,512]{1,0:T(8,128)S(1)}, f32[5,512]{1,0:T(8,128)S(1)}, u32[]{:S(2)}, u32[]{:S(2)}) collective-permute-start(f32[5,512]{1,0:T(8,128)S(1)} %get-tuple-element.1136), channel_id=1, source_target_pairs={{0,32},{32,64},{64,96},{96,128},{128,160},{160,192},{192,224},{224... | collective-permute-start | bytes 30728 | tf_op jit(solution)/shard_map/while/body/eval_jaxpr/ppermute | solution.py:26
  144.5 1.4 collective-permute-done
  146.5 5.4 %collective-permute-start = (f32[5,512]{1,0:T(8,128)S(1)}, f32[5,512]{1,0:T(8,128)S(1)}, u32[]{:S(2)}, u32[]{:S(2)}) collective-permute-start(f32[5,512]{1,0:T(8,128)S(1)} %get-tuple-element.1136), channel_id=1, source_target_pairs={{0,32},{32,64},{64,96},{96,128},{128,160},{160,192},{192,224},{224... | collective-permute-start | bytes 30728 | tf_op jit(solution)/shard_map/while/body/eval_jaxpr/ppermute | solution.py:26
  153.9 5.4 %collective-permute-start = (f32[5,512]{1,0:T(8,128)S(1)}, f32[5,512]{1,0:T(8,128)S(1)}, u32[]{:S(2)}, u32[]{:S(2)}) collective-permute-start(f32[5,512]{1,0:T(8,128)S(1)} %get-tuple-element.1136), channel_id=1, source_target_pairs={{0,32},{32,64},{64,96},{96,128},{128,160},{160,192},{192,224},{224... | collective-permute-start | bytes 30728 | tf_op jit(solution)/shard_map/while/body/eval_jaxpr/ppermute | solution.py:26
  159.4 1.4 collective-permute-done
  161.4 5.4 %collective-permute-start = (f32[5,512]{1,0:T(8,128)S(1)}, f32[5,512]{1,0:T(8,128)S(1)}, u32[]{:S(2)}, u32[]{:S(2)}) collective-permute-start(f32[5,512]{1,0:T(8,128)S(1)} %get-tuple-element.1136), channel_id=1, source_target_pairs={{0,32},{32,64},{64,96},{96,128},{128,160},{160,192},{192,224},{224... | collective-permute-start | bytes 30728 | tf_op jit(solution)/shard_map/while/body/eval_jaxpr/ppermute | solution.py:26
  168.8 5.4 %collective-permute-start = (f32[5,512]{1,0:T(8,128)S(1)}, f32[5,512]{1,0:T(8,128)S(1)}, u32[]{:S(2)}, u32[]{:S(2)}) collective-permute-start(f32[5,512]{1,0:T(8,128)S(1)} %get-tuple-element.1136), channel_id=1, source_target_pairs={{0,32},{32,64},{64,96},{96,128},{128,160},{160,192},{192,224},{224... | collective-permute-start | bytes 30728 | tf_op jit(solution)/shard_map/while/body/eval_jaxpr/ppermute | solution.py:26
  176.3 5.4 %collective-permute-start = (f32[5,512]{1,0:T(8,128)S(1)}, f32[5,512]{1,0:T(8,128)S(1)}, u32[]{:S(2)}, u32[]{:S(2)}) collective-permute-start(f32[5,512]{1,0:T(8,128)S(1)} %get-tuple-element.1136), channel_id=1, source_target_pairs={{0,32},{32,64},{64,96},{96,128},{128,160},{160,192},{192,224},{224... | collective-permute-start | bytes 30728 | tf_op jit(solution)/shard_map/while/body/eval_jaxpr/ppermute | solution.py:26
  183.7 5.4 %collective-permute-start = (f32[5,512]{1,0:T(8,128)S(1)}, f32[5,512]{1,0:T(8,128)S(1)}, u32[]{:S(2)}, u32[]{:S(2)}) collective-permute-start(f32[5,512]{1,0:T(8,128)S(1)} %get-tuple-element.1136), channel_id=1, source_target_pairs={{0,32},{32,64},{64,96},{96,128},{128,160},{160,192},{192,224},{224... | collective-permute-start | bytes 30728 | tf_op jit(solution)/shard_map/while/body/eval_jaxpr/ppermute | solution.py:26
  191.1 59.8 %while.92 = (s32[]{:T(128)}, f32[5,512]{1,0:T(8,128)}, f32[5,16,512]{2,1,0:T(8,128)S(1)}, f32[5,5,16,512]{3,2,1,0:T(8,128)S(1)}, f32[5,16,512]{2,0,1:T(8,128)S(1...) while((s32[]{:T(128)}, f32[5,512]{1,0:T(8,128)}, ...), condition=%wide.region_13.14_spmd, body=%wide.region_10.13_spmd.sunk | while | flops 51202 | bytes 460949 | solution.py:102
  251.1 40.7 %while.96 = (s32[]{:T(128)}, f32[5,5,512]{2,1,0:T(8,128)S(1)}, f32[5,512]{1,0:T(8,128)S(1)}, f32[5,5,16,512]{3,1,0,2:T(8,128)S(1)}, f32[5,5,16,512]{3,2,1,0:T(8,...) while((s32[]{:T(128)}, f32[5,5,512]{2,1,0:T(8,128)S(1)}, ...), condition=%wide.region_18.19_spmd.clone, body=%wide.region_14.18_spmd.clone.sunk | while | flops 271367 | bytes 860353 | solution.py:115
  292.4 111.8 %while.93 = (s32[]{:T(128)}, f32[5,512]{1,0:T(8,128)S(1)}, f32[5,512]{1,0:T(8,128)}, f32[5,5,512]{2,1,0:T(8,128)S(1)}, f32[5,512]{1,0:T(8,128)S(1)}, /*index=5*/s32[]{:T(128)}) while((s32[]{:T(128)}, f32[5,512]{1,0:T(8,128)S(1)}, f32[5,512]{1,0:T(8,128)}, f32[5,5,512]{2,1,0:T(8,128)S(1)}, f32[5,512]{1,0:T(8,128)S(1)}, ...), condition=%wide.region_21.22_spmd, body=%wide.region_19.21_spmd.sunk | while | flops 25602 | bytes 184457 | solution.py:122
  292.4 1.9 collective-permute-start.1
  294.3 5.2 %collective-permute-done.1 = f32[5,512]{1,0:T(8,128)S(1)} collective-permute-done((f32[5,512]{1,0:T(8,128)S(1)}, f32[5,512]{1,0:T(8,128)S(1)}, u32[]{:S(2)}, u32[]{:S(2)}) %collective-permute-start.1) | collective-permute-done | bytes 10272 | tf_op jit(solution)/shard_map/while/body/eval_jaxpr/ppermute | solution.py:26
  300.1 1.9 collective-permute-start.1
  302.0 4.9 %collective-permute-done.1 = f32[5,512]{1,0:T(8,128)S(1)} collective-permute-done((f32[5,512]{1,0:T(8,128)S(1)}, f32[5,512]{1,0:T(8,128)S(1)}, u32[]{:S(2)}, u32[]{:S(2)}) %collective-permute-start.1) | collective-permute-done | bytes 10272 | tf_op jit(solution)/shard_map/while/body/eval_jaxpr/ppermute | solution.py:26
  307.5 1.9 collective-permute-start.1
  309.4 4.9 %collective-permute-done.1 = f32[5,512]{1,0:T(8,128)S(1)} collective-permute-done((f32[5,512]{1,0:T(8,128)S(1)}, f32[5,512]{1,0:T(8,128)S(1)}, u32[]{:S(2)}, u32[]{:S(2)}) %collective-permute-start.1) | collective-permute-done | bytes 10272 | tf_op jit(solution)/shard_map/while/body/eval_jaxpr/ppermute | solution.py:26
  315.0 1.9 collective-permute-start.1
  316.9 4.9 %collective-permute-done.1 = f32[5,512]{1,0:T(8,128)S(1)} collective-permute-done((f32[5,512]{1,0:T(8,128)S(1)}, f32[5,512]{1,0:T(8,128)S(1)}, u32[]{:S(2)}, u32[]{:S(2)}) %collective-permute-start.1) | collective-permute-done | bytes 10272 | tf_op jit(solution)/shard_map/while/body/eval_jaxpr/ppermute | solution.py:26
  322.4 1.9 collective-permute-start.1
  324.3 4.9 %collective-permute-done.1 = f32[5,512]{1,0:T(8,128)S(1)} collective-permute-done((f32[5,512]{1,0:T(8,128)S(1)}, f32[5,512]{1,0:T(8,128)S(1)}, u32[]{:S(2)}, u32[]{:S(2)}) %collective-permute-start.1) | collective-permute-done | bytes 10272 | tf_op jit(solution)/shard_map/while/body/eval_jaxpr/ppermute | solution.py:26
  329.8 1.9 collective-permute-start.1
  331.7 4.9 %collective-permute-done.1 = f32[5,512]{1,0:T(8,128)S(1)} collective-permute-done((f32[5,512]{1,0:T(8,128)S(1)}, f32[5,512]{1,0:T(8,128)S(1)}, u32[]{:S(2)}, u32[]{:S(2)}) %collective-permute-start.1) | collective-permute-done | bytes 10272 | tf_op jit(solution)/shard_map/while/body/eval_jaxpr/ppermute | solution.py:26
  337.3 1.9 collective-permute-start.1
  339.2 4.9 %collective-permute-done.1 = f32[5,512]{1,0:T(8,128)S(1)} collective-permute-done((f32[5,512]{1,0:T(8,128)S(1)}, f32[5,512]{1,0:T(8,128)S(1)}, u32[]{:S(2)}, u32[]{:S(2)}) %collective-permute-start.1) | collective-permute-done | bytes 10272 | tf_op jit(solution)/shard_map/while/body/eval_jaxpr/ppermute | solution.py:26
  344.7 1.9 collective-permute-start.1
  346.6 4.9 %collective-permute-done.1 = f32[5,512]{1,0:T(8,128)S(1)} collective-permute-done((f32[5,512]{1,0:T(8,128)S(1)}, f32[5,512]{1,0:T(8,128)S(1)}, u32[]{:S(2)}, u32[]{:S(2)}) %collective-permute-start.1) | collective-permute-done | bytes 10272 | tf_op jit(solution)/shard_map/while/body/eval_jaxpr/ppermute | solution.py:26
  352.1 1.9 collective-permute-start.1
  354.1 4.9 %collective-permute-done.1 = f32[5,512]{1,0:T(8,128)S(1)} collective-permute-done((f32[5,512]{1,0:T(8,128)S(1)}, f32[5,512]{1,0:T(8,128)S(1)}, u32[]{:S(2)}, u32[]{:S(2)}) %collective-permute-start.1) | collective-permute-done | bytes 10272 | tf_op jit(solution)/shard_map/while/body/eval_jaxpr/ppermute | solution.py:26
  359.6 1.9 collective-permute-start.1
  361.5 4.9 %collective-permute-done.1 = f32[5,512]{1,0:T(8,128)S(1)} collective-permute-done((f32[5,512]{1,0:T(8,128)S(1)}, f32[5,512]{1,0:T(8,128)S(1)}, u32[]{:S(2)}, u32[]{:S(2)}) %collective-permute-start.1) | collective-permute-done | bytes 10272 | tf_op jit(solution)/shard_map/while/body/eval_jaxpr/ppermute | solution.py:26
  367.0 1.9 collective-permute-start.1
  368.9 4.9 %collective-permute-done.1 = f32[5,512]{1,0:T(8,128)S(1)} collective-permute-done((f32[5,512]{1,0:T(8,128)S(1)}, f32[5,512]{1,0:T(8,128)S(1)}, u32[]{:S(2)}, u32[]{:S(2)}) %collective-permute-start.1) | collective-permute-done | bytes 10272 | tf_op jit(solution)/shard_map/while/body/eval_jaxpr/ppermute | solution.py:26
  374.5 1.9 collective-permute-start.1
  376.4 4.9 %collective-permute-done.1 = f32[5,512]{1,0:T(8,128)S(1)} collective-permute-done((f32[5,512]{1,0:T(8,128)S(1)}, f32[5,512]{1,0:T(8,128)S(1)}, u32[]{:S(2)}, u32[]{:S(2)}) %collective-permute-start.1) | collective-permute-done | bytes 10272 | tf_op jit(solution)/shard_map/while/body/eval_jaxpr/ppermute | solution.py:26
  381.9 1.9 collective-permute-start.1
  383.8 4.9 %collective-permute-done.1 = f32[5,512]{1,0:T(8,128)S(1)} collective-permute-done((f32[5,512]{1,0:T(8,128)S(1)}, f32[5,512]{1,0:T(8,128)S(1)}, u32[]{:S(2)}, u32[]{:S(2)}) %collective-permute-start.1) | collective-permute-done | bytes 10272 | tf_op jit(solution)/shard_map/while/body/eval_jaxpr/ppermute | solution.py:26
  389.3 1.9 collective-permute-start.1
  391.2 4.9 %collective-permute-done.1 = f32[5,512]{1,0:T(8,128)S(1)} collective-permute-done((f32[5,512]{1,0:T(8,128)S(1)}, f32[5,512]{1,0:T(8,128)S(1)}, u32[]{:S(2)}, u32[]{:S(2)}) %collective-permute-start.1) | collective-permute-done | bytes 10272 | tf_op jit(solution)/shard_map/while/body/eval_jaxpr/ppermute | solution.py:26
  396.8 1.9 collective-permute-start.1
  398.7 4.9 %collective-permute-done.1 = f32[5,512]{1,0:T(8,128)S(1)} collective-permute-done((f32[5,512]{1,0:T(8,128)S(1)}, f32[5,512]{1,0:T(8,128)S(1)}, u32[]{:S(2)}, u32[]{:S(2)}) %collective-permute-start.1) | collective-permute-done | bytes 10272 | tf_op jit(solution)/shard_map/while/body/eval_jaxpr/ppermute | solution.py:26
  404.2 61.9 %while.94 = (s32[]{:T(128)}, f32[5,512]{1,0:T(8,128)}, f32[5,16,512]{2,1,0:T(8,128)S(1)}, f32[5,16,512]{2,1,0:T(8,128)S(1)}, f32[5,5,16,512]{3,2,1,0:T(8,128)S(1...) while((s32[]{:T(128)}, f32[5,512]{1,0:T(8,128)}, ...), condition=%wide.region_25.26_spmd, body=%wide.region_22.25_spmd.sunk | while | flops 53766 | bytes 460983 | solution.py:134
  (771 shorter events, 231.3 us)
Async XLA Ops:
  0.0 37.6 %copy-start.2 = (f32[25,16,512]{2,1,0:T(8,128)S(1)}, f32[25,16,512]{2,1,0:T(8,128)}, u32[]{:S(2)}) copy-start(f32[25,16,512]{2,1,0:T(8,128)} %param.24) | copy-start | bytes 2457604
  1.1 37.0 %collective-permute-start.2 = (f32[5,16,128]{2,0,1:T(8,128)S(1)}, f32[5,16,128]{2,0,1:T(8,128)S(1)}, u32[]{:S(2)}, u32[]{:S(2)}) collective-permute-start(f32[5,16,128]{2,0,1:T(8,128)S(1)} %get-tuple-element.850), channel_id=1, source_target_pairs={{1,0},{2,1},{3,2},{4,3},{5,4},{6,5},{7,6},{8,7},{9,8},{10,9},{11,1... | collective-permute-start | bytes 122888 | tf_op jit(solution)/shard_map/ppermute | solution.py:18
  7.7 30.5 %collective-permute-start.3 = (f32[5,16,128]{2,0,1:T(8,128)S(1)}, f32[5,16,128]{2,0,1:T(8,128)S(1)}, u32[]{:S(2)}, u32[]{:S(2)}) collective-permute-start(f32[5,16,128]{2,0,1:T(8,128)S(1)} %get-tuple-element.851), channel_id=1, source_target_pairs={{0,1},{1,2},{2,3},{3,4},{4,5},{5,6},{6,7},{7,8},{8,9},{9,10},{10,1... | collective-permute-start | bytes 122888 | tf_op jit(solution)/shard_map/ppermute | solution.py:15
  35.8 2.4 copy-start.5
  35.8 2.3 copy-start.6
  79.9 6.5 %collective-permute-start = (f32[5,512]{1,0:T(8,128)S(1)}, f32[5,512]{1,0:T(8,128)S(1)}, u32[]{:S(2)}, u32[]{:S(2)}) collective-permute-start(f32[5,512]{1,0:T(8,128)S(1)} %get-tuple-element.1136), channel_id=1, source_target_pairs={{0,32},{32,64},{64,96},{96,128},{128,160},{160,192},{192,224},{224... | collective-permute-start | bytes 30728 | tf_op jit(solution)/shard_map/while/body/eval_jaxpr/ppermute | solution.py:26
  86.9 6.8 %collective-permute-start = (f32[5,512]{1,0:T(8,128)S(1)}, f32[5,512]{1,0:T(8,128)S(1)}, u32[]{:S(2)}, u32[]{:S(2)}) collective-permute-start(f32[5,512]{1,0:T(8,128)S(1)} %get-tuple-element.1136), channel_id=1, source_target_pairs={{0,32},{32,64},{64,96},{96,128},{128,160},{160,192},{192,224},{224... | collective-permute-start | bytes 30728 | tf_op jit(solution)/shard_map/while/body/eval_jaxpr/ppermute | solution.py:26
  94.3 6.8 %collective-permute-start = (f32[5,512]{1,0:T(8,128)S(1)}, f32[5,512]{1,0:T(8,128)S(1)}, u32[]{:S(2)}, u32[]{:S(2)}) collective-permute-start(f32[5,512]{1,0:T(8,128)S(1)} %get-tuple-element.1136), channel_id=1, source_target_pairs={{0,32},{32,64},{64,96},{96,128},{128,160},{160,192},{192,224},{224... | collective-permute-start | bytes 30728 | tf_op jit(solution)/shard_map/while/body/eval_jaxpr/ppermute | solution.py:26
  101.8 6.8 %collective-permute-start = (f32[5,512]{1,0:T(8,128)S(1)}, f32[5,512]{1,0:T(8,128)S(1)}, u32[]{:S(2)}, u32[]{:S(2)}) collective-permute-start(f32[5,512]{1,0:T(8,128)S(1)} %get-tuple-element.1136), channel_id=1, source_target_pairs={{0,32},{32,64},{64,96},{96,128},{128,160},{160,192},{192,224},{224... | collective-permute-start | bytes 30728 | tf_op jit(solution)/shard_map/while/body/eval_jaxpr/ppermute | solution.py:26
  109.2 6.8 %collective-permute-start = (f32[5,512]{1,0:T(8,128)S(1)}, f32[5,512]{1,0:T(8,128)S(1)}, u32[]{:S(2)}, u32[]{:S(2)}) collective-permute-start(f32[5,512]{1,0:T(8,128)S(1)} %get-tuple-element.1136), channel_id=1, source_target_pairs={{0,32},{32,64},{64,96},{96,128},{128,160},{160,192},{192,224},{224... | collective-permute-start | bytes 30728 | tf_op jit(solution)/shard_map/while/body/eval_jaxpr/ppermute | solution.py:26
  116.7 6.8 %collective-permute-start = (f32[5,512]{1,0:T(8,128)S(1)}, f32[5,512]{1,0:T(8,128)S(1)}, u32[]{:S(2)}, u32[]{:S(2)}) collective-permute-start(f32[5,512]{1,0:T(8,128)S(1)} %get-tuple-element.1136), channel_id=1, source_target_pairs={{0,32},{32,64},{64,96},{96,128},{128,160},{160,192},{192,224},{224... | collective-permute-start | bytes 30728 | tf_op jit(solution)/shard_map/while/body/eval_jaxpr/ppermute | solution.py:26
  124.1 6.9 %collective-permute-start = (f32[5,512]{1,0:T(8,128)S(1)}, f32[5,512]{1,0:T(8,128)S(1)}, u32[]{:S(2)}, u32[]{:S(2)}) collective-permute-start(f32[5,512]{1,0:T(8,128)S(1)} %get-tuple-element.1136), channel_id=1, source_target_pairs={{0,32},{32,64},{64,96},{96,128},{128,160},{160,192},{192,224},{224... | collective-permute-start | bytes 30728 | tf_op jit(solution)/shard_map/while/body/eval_jaxpr/ppermute | solution.py:26
  131.6 6.8 %collective-permute-start = (f32[5,512]{1,0:T(8,128)S(1)}, f32[5,512]{1,0:T(8,128)S(1)}, u32[]{:S(2)}, u32[]{:S(2)}) collective-permute-start(f32[5,512]{1,0:T(8,128)S(1)} %get-tuple-element.1136), channel_id=1, source_target_pairs={{0,32},{32,64},{64,96},{96,128},{128,160},{160,192},{192,224},{224... | collective-permute-start | bytes 30728 | tf_op jit(solution)/shard_map/while/body/eval_jaxpr/ppermute | solution.py:26
  139.1 6.8 %collective-permute-start = (f32[5,512]{1,0:T(8,128)S(1)}, f32[5,512]{1,0:T(8,128)S(1)}, u32[]{:S(2)}, u32[]{:S(2)}) collective-permute-start(f32[5,512]{1,0:T(8,128)S(1)} %get-tuple-element.1136), channel_id=1, source_target_pairs={{0,32},{32,64},{64,96},{96,128},{128,160},{160,192},{192,224},{224... | collective-permute-start | bytes 30728 | tf_op jit(solution)/shard_map/while/body/eval_jaxpr/ppermute | solution.py:26
  146.5 6.8 %collective-permute-start = (f32[5,512]{1,0:T(8,128)S(1)}, f32[5,512]{1,0:T(8,128)S(1)}, u32[]{:S(2)}, u32[]{:S(2)}) collective-permute-start(f32[5,512]{1,0:T(8,128)S(1)} %get-tuple-element.1136), channel_id=1, source_target_pairs={{0,32},{32,64},{64,96},{96,128},{128,160},{160,192},{192,224},{224... | collective-permute-start | bytes 30728 | tf_op jit(solution)/shard_map/while/body/eval_jaxpr/ppermute | solution.py:26
  153.9 6.8 %collective-permute-start = (f32[5,512]{1,0:T(8,128)S(1)}, f32[5,512]{1,0:T(8,128)S(1)}, u32[]{:S(2)}, u32[]{:S(2)}) collective-permute-start(f32[5,512]{1,0:T(8,128)S(1)} %get-tuple-element.1136), channel_id=1, source_target_pairs={{0,32},{32,64},{64,96},{96,128},{128,160},{160,192},{192,224},{224... | collective-permute-start | bytes 30728 | tf_op jit(solution)/shard_map/while/body/eval_jaxpr/ppermute | solution.py:26
  161.4 6.8 %collective-permute-start = (f32[5,512]{1,0:T(8,128)S(1)}, f32[5,512]{1,0:T(8,128)S(1)}, u32[]{:S(2)}, u32[]{:S(2)}) collective-permute-start(f32[5,512]{1,0:T(8,128)S(1)} %get-tuple-element.1136), channel_id=1, source_target_pairs={{0,32},{32,64},{64,96},{96,128},{128,160},{160,192},{192,224},{224... | collective-permute-start | bytes 30728 | tf_op jit(solution)/shard_map/while/body/eval_jaxpr/ppermute | solution.py:26
  168.8 6.8 %collective-permute-start = (f32[5,512]{1,0:T(8,128)S(1)}, f32[5,512]{1,0:T(8,128)S(1)}, u32[]{:S(2)}, u32[]{:S(2)}) collective-permute-start(f32[5,512]{1,0:T(8,128)S(1)} %get-tuple-element.1136), channel_id=1, source_target_pairs={{0,32},{32,64},{64,96},{96,128},{128,160},{160,192},{192,224},{224... | collective-permute-start | bytes 30728 | tf_op jit(solution)/shard_map/while/body/eval_jaxpr/ppermute | solution.py:26
  176.3 6.8 %collective-permute-start = (f32[5,512]{1,0:T(8,128)S(1)}, f32[5,512]{1,0:T(8,128)S(1)}, u32[]{:S(2)}, u32[]{:S(2)}) collective-permute-start(f32[5,512]{1,0:T(8,128)S(1)} %get-tuple-element.1136), channel_id=1, source_target_pairs={{0,32},{32,64},{64,96},{96,128},{128,160},{160,192},{192,224},{224... | collective-permute-start | bytes 30728 | tf_op jit(solution)/shard_map/while/body/eval_jaxpr/ppermute | solution.py:26
  183.7 6.8 %collective-permute-start = (f32[5,512]{1,0:T(8,128)S(1)}, f32[5,512]{1,0:T(8,128)S(1)}, u32[]{:S(2)}, u32[]{:S(2)}) collective-permute-start(f32[5,512]{1,0:T(8,128)S(1)} %get-tuple-element.1136), channel_id=1, source_target_pairs={{0,32},{32,64},{64,96},{96,128},{128,160},{160,192},{192,224},{224... | collective-permute-start | bytes 30728 | tf_op jit(solution)/shard_map/while/body/eval_jaxpr/ppermute | solution.py:26
  194.3 0.6 copy-start.1
  198.0 0.6 copy-start.1
  201.8 0.6 copy-start.1
  205.5 0.6 copy-start.1
  209.3 0.6 copy-start.1
  213.0 0.6 copy-start.1
  216.7 0.6 copy-start.1
  220.5 0.6 copy-start.1
  224.2 0.6 copy-start.1
  227.9 0.6 copy-start.1
  231.7 0.6 copy-start.1
  235.4 0.6 copy-start.1
  239.2 0.6 copy-start.1
  242.9 0.6 copy-start.1
  246.6 0.6 copy-start.1
  250.4 0.6 copy-start.1
  292.4 7.1 %collective-permute-start.1 = (f32[5,512]{1,0:T(8,128)S(1)}, f32[5,512]{1,0:T(8,128)S(1)}, u32[]{:S(2)}, u32[]{:S(2)}) collective-permute-start(f32[5,512]{1,0:T(8,128)S(1)} %get-tuple-element.1214), channel_id=1, source_target_pairs={{32,0},{64,32},{96,64},{128,96},{160,128},{192,160},{224,192},{256... | collective-permute-start | bytes 30728 | tf_op jit(solution)/shard_map/while/body/eval_jaxpr/ppermute | solution.py:26
  299.5 0.6 copy-start.3
  300.1 6.8 %collective-permute-start.1 = (f32[5,512]{1,0:T(8,128)S(1)}, f32[5,512]{1,0:T(8,128)S(1)}, u32[]{:S(2)}, u32[]{:S(2)}) collective-permute-start(f32[5,512]{1,0:T(8,128)S(1)} %get-tuple-element.1214), channel_id=1, source_target_pairs={{32,0},{64,32},{96,64},{128,96},{160,128},{192,160},{224,192},{256... | collective-permute-start | bytes 30728 | tf_op jit(solution)/shard_map/while/body/eval_jaxpr/ppermute | solution.py:26
  306.9 0.6 copy-start.3
  307.5 6.8 %collective-permute-start.1 = (f32[5,512]{1,0:T(8,128)S(1)}, f32[5,512]{1,0:T(8,128)S(1)}, u32[]{:S(2)}, u32[]{:S(2)}) collective-permute-start(f32[5,512]{1,0:T(8,128)S(1)} %get-tuple-element.1214), channel_id=1, source_target_pairs={{32,0},{64,32},{96,64},{128,96},{160,128},{192,160},{224,192},{256... | collective-permute-start | bytes 30728 | tf_op jit(solution)/shard_map/while/body/eval_jaxpr/ppermute | solution.py:26
  314.3 0.6 copy-start.3
  315.0 6.8 %collective-permute-start.1 = (f32[5,512]{1,0:T(8,128)S(1)}, f32[5,512]{1,0:T(8,128)S(1)}, u32[]{:S(2)}, u32[]{:S(2)}) collective-permute-start(f32[5,512]{1,0:T(8,128)S(1)} %get-tuple-element.1214), channel_id=1, source_target_pairs={{32,0},{64,32},{96,64},{128,96},{160,128},{192,160},{224,192},{256... | collective-permute-start | bytes 30728 | tf_op jit(solution)/shard_map/while/body/eval_jaxpr/ppermute | solution.py:26
  321.8 0.6 copy-start.3
  322.4 6.8 %collective-permute-start.1 = (f32[5,512]{1,0:T(8,128)S(1)}, f32[5,512]{1,0:T(8,128)S(1)}, u32[]{:S(2)}, u32[]{:S(2)}) collective-permute-start(f32[5,512]{1,0:T(8,128)S(1)} %get-tuple-element.1214), channel_id=1, source_target_pairs={{32,0},{64,32},{96,64},{128,96},{160,128},{192,160},{224,192},{256... | collective-permute-start | bytes 30728 | tf_op jit(solution)/shard_map/while/body/eval_jaxpr/ppermute | solution.py:26
  329.2 0.6 copy-start.3
  329.8 6.8 %collective-permute-start.1 = (f32[5,512]{1,0:T(8,128)S(1)}, f32[5,512]{1,0:T(8,128)S(1)}, u32[]{:S(2)}, u32[]{:S(2)}) collective-permute-start(f32[5,512]{1,0:T(8,128)S(1)} %get-tuple-element.1214), channel_id=1, source_target_pairs={{32,0},{64,32},{96,64},{128,96},{160,128},{192,160},{224,192},{256... | collective-permute-start | bytes 30728 | tf_op jit(solution)/shard_map/while/body/eval_jaxpr/ppermute | solution.py:26
  336.7 0.6 copy-start.3
  337.3 6.8 %collective-permute-start.1 = (f32[5,512]{1,0:T(8,128)S(1)}, f32[5,512]{1,0:T(8,128)S(1)}, u32[]{:S(2)}, u32[]{:S(2)}) collective-permute-start(f32[5,512]{1,0:T(8,128)S(1)} %get-tuple-element.1214), channel_id=1, source_target_pairs={{32,0},{64,32},{96,64},{128,96},{160,128},{192,160},{224,192},{256... | collective-permute-start | bytes 30728 | tf_op jit(solution)/shard_map/while/body/eval_jaxpr/ppermute | solution.py:26
  344.1 0.6 copy-start.3
  344.7 6.8 %collective-permute-start.1 = (f32[5,512]{1,0:T(8,128)S(1)}, f32[5,512]{1,0:T(8,128)S(1)}, u32[]{:S(2)}, u32[]{:S(2)}) collective-permute-start(f32[5,512]{1,0:T(8,128)S(1)} %get-tuple-element.1214), channel_id=1, source_target_pairs={{32,0},{64,32},{96,64},{128,96},{160,128},{192,160},{224,192},{256... | collective-permute-start | bytes 30728 | tf_op jit(solution)/shard_map/while/body/eval_jaxpr/ppermute | solution.py:26
  351.5 0.6 copy-start.3
  352.1 6.8 %collective-permute-start.1 = (f32[5,512]{1,0:T(8,128)S(1)}, f32[5,512]{1,0:T(8,128)S(1)}, u32[]{:S(2)}, u32[]{:S(2)}) collective-permute-start(f32[5,512]{1,0:T(8,128)S(1)} %get-tuple-element.1214), channel_id=1, source_target_pairs={{32,0},{64,32},{96,64},{128,96},{160,128},{192,160},{224,192},{256... | collective-permute-start | bytes 30728 | tf_op jit(solution)/shard_map/while/body/eval_jaxpr/ppermute | solution.py:26
  359.0 0.6 copy-start.3
  359.6 6.8 %collective-permute-start.1 = (f32[5,512]{1,0:T(8,128)S(1)}, f32[5,512]{1,0:T(8,128)S(1)}, u32[]{:S(2)}, u32[]{:S(2)}) collective-permute-start(f32[5,512]{1,0:T(8,128)S(1)} %get-tuple-element.1214), channel_id=1, source_target_pairs={{32,0},{64,32},{96,64},{128,96},{160,128},{192,160},{224,192},{256... | collective-permute-start | bytes 30728 | tf_op jit(solution)/shard_map/while/body/eval_jaxpr/ppermute | solution.py:26
  366.4 0.6 copy-start.3
  367.0 6.8 %collective-permute-start.1 = (f32[5,512]{1,0:T(8,128)S(1)}, f32[5,512]{1,0:T(8,128)S(1)}, u32[]{:S(2)}, u32[]{:S(2)}) collective-permute-start(f32[5,512]{1,0:T(8,128)S(1)} %get-tuple-element.1214), channel_id=1, source_target_pairs={{32,0},{64,32},{96,64},{128,96},{160,128},{192,160},{224,192},{256... | collective-permute-start | bytes 30728 | tf_op jit(solution)/shard_map/while/body/eval_jaxpr/ppermute | solution.py:26
  373.8 0.6 copy-start.3
  374.5 6.8 %collective-permute-start.1 = (f32[5,512]{1,0:T(8,128)S(1)}, f32[5,512]{1,0:T(8,128)S(1)}, u32[]{:S(2)}, u32[]{:S(2)}) collective-permute-start(f32[5,512]{1,0:T(8,128)S(1)} %get-tuple-element.1214), channel_id=1, source_target_pairs={{32,0},{64,32},{96,64},{128,96},{160,128},{192,160},{224,192},{256... | collective-permute-start | bytes 30728 | tf_op jit(solution)/shard_map/while/body/eval_jaxpr/ppermute | solution.py:26
  381.3 0.6 copy-start.3
  381.9 6.8 %collective-permute-start.1 = (f32[5,512]{1,0:T(8,128)S(1)}, f32[5,512]{1,0:T(8,128)S(1)}, u32[]{:S(2)}, u32[]{:S(2)}) collective-permute-start(f32[5,512]{1,0:T(8,128)S(1)} %get-tuple-element.1214), channel_id=1, source_target_pairs={{32,0},{64,32},{96,64},{128,96},{160,128},{192,160},{224,192},{256... | collective-permute-start | bytes 30728 | tf_op jit(solution)/shard_map/while/body/eval_jaxpr/ppermute | solution.py:26
  389.3 6.8 %collective-permute-start.1 = (f32[5,512]{1,0:T(8,128)S(1)}, f32[5,512]{1,0:T(8,128)S(1)}, u32[]{:S(2)}, u32[]{:S(2)}) collective-permute-start(f32[5,512]{1,0:T(8,128)S(1)} %get-tuple-element.1214), channel_id=1, source_target_pairs={{32,0},{64,32},{96,64},{128,96},{160,128},{192,160},{224,192},{256... | collective-permute-start | bytes 30728 | tf_op jit(solution)/shard_map/while/body/eval_jaxpr/ppermute | solution.py:26
  396.8 6.8 %collective-permute-start.1 = (f32[5,512]{1,0:T(8,128)S(1)}, f32[5,512]{1,0:T(8,128)S(1)}, u32[]{:S(2)}, u32[]{:S(2)}) collective-permute-start(f32[5,512]{1,0:T(8,128)S(1)} %get-tuple-element.1214), channel_id=1, source_target_pairs={{32,0},{64,32},{96,64},{128,96},{160,128},{192,160},{224,192},{256... | collective-permute-start | bytes 30728 | tf_op jit(solution)/shard_map/while/body/eval_jaxpr/ppermute | solution.py:26
  404.2 61.9 %copy-start.4 = (f32[5,16,512]{2,1,0:T(8,128)S(1)}, f32[5,16,512]{2,1,0:T(8,128)}, u32[]{:S(2)}) copy-start(f32[5,16,512]{2,1,0:T(8,128)} %param.21) | copy-start | bytes 491524
  (18 other events, 10.9 us)
where the time goes:
time: 473 us; the launch traced here: 467 us
  local copies, waits for them, and re-layouts  140 us (30%)
  starting transfers between devices  118 us (25%)
  waiting for transfers between devices  95.3 us (20%)
  other arithmetic  84.3 us (18%)
  blocking collectives  24.3 us (5%)
  loops' own time  4.86 us (1%)
    ppermute x30, starting transfers between devices, passed_along(): lax.ppermute(value, axis, [(source, source + steps) for source in range(f...  109 us
    ppermute x30, waiting for transfers between devices, passed_along(): lax.ppermute(value, axis, [(source, source + steps) for source in range(f...  95.3 us
    reduce_sum x143, other arithmetic, apply_block(): return jnp.sum(matrix * vector[None, :, :], axis=1)  27.7 us
    while x124, local copies, waits for them, and re-layouts  24.7 us
    all_gather x1, blocking collectives, local(): rotor_cells = lax.all_gather(rotor_plane, 'pitch', axis=1, tiled=True)  24.3 us
    dynamic_slice x16, local copies, waits for them, and re-layouts, backward_sweep(): up_now = lax.dynamic_index_in_dim(upper_blocks, plane, 2, keepdims=False)  17.4 us
    dynamic_slice x16, local copies, waits for them, and re-layouts, forward_sweep(): low_now = lax.dynamic_index_in_dim(lower_blocks, plane, 2, keepdims=False)  17.3 us
    dynamic_slice x16, local copies, waits for them, and re-layouts, forward_map(): lax.dynamic_index_in_dim(lower_blocks, plane, 2, keepdims=False)  16.8 us
  transfers between devices with their start and end apart: 32, of which 30 were waited for; matrix products, arithmetic and copies ran while one was open for 1% of the time, Pallas kernels for 0%

commit v1 on v0

v1 whole, which is shorter than its diff:
```python
import jax
import jax.numpy as jnp
from jax import lax
from jax.experimental import pallas as pl
from jax.experimental.pallas import tpu as pltpu
from jax.sharding import PartitionSpec as P

MESH = pl.DeviceIdType.MESH
NC = 5
NS = 16
NPI = 32
CUT = 8
HOPS = 8


def mm(a, b):
    return jnp.stack([sum(a[r, k][None] * b[k] for k in range(NC)) for r in range(NC)])


def mv(a, x):
    return sum(a[:, k] * x[k][None] for k in range(NC))


def kernel(
    flow, res, spr, dinv, low, upp, partner, out,
    flow_v, res_v, spr_v, d_v, l_v, u_v, src_v,
    s_v, t_v, f_v, q_v, p_v, c_v,
    halo_lo, halo_hi, rot, rots, ghost,
    m_d, b_d, w_d, v_d, ww_d, vh, fsend, frecv, bsend, brecv,
    part_s, ld_sem, hs_sem, hr_sem, gs_sem, gr_sem, fs_sem, fr_sem, bs_sem, br_sem,
):
    st = lax.axis_index("stream")
    pt = lax.axis_index("pitch")
    up_s, dn_s = lax.rem(st + 1, NS), lax.rem(st + NS - 1, NS)
    up_p, dn_p = lax.rem(pt + 1, NPI), lax.rem(pt + NPI - 1, NPI)
    is_cut = st == CUT

    loads = [
        pltpu.make_async_copy(h, v, ld_sem.at[i])
        for i, (h, v) in enumerate(
            ((flow, flow_v), (dinv, d_v), (low, l_v), (upp, u_v), (res, res_v), (spr, spr_v))
        )
    ]
    for c in loads:
        c.start()

    barrier = pltpu.get_barrier_semaphore()
    for nb in (up_s, dn_s):
        pl.semaphore_signal(barrier, inc=1, device_id={"stream": nb}, device_id_type=MESH)
    for nb in (up_p, dn_p):
        pl.semaphore_signal(barrier, inc=1, device_id={"pitch": nb}, device_id_type=MESH)

    @pl.when(is_cut)
    def _():
        for d in range(2, NPI - 1):
            pl.semaphore_signal(
                barrier, inc=1, device_id={"pitch": lax.rem(pt + d, NPI)}, device_id_type=MESH
            )

    pl.semaphore_wait(barrier, jnp.where(is_cut, NPI + 1, 4))

    loads[0].wait()

    def halos():
        copies = []
        for h in range(2):
            copies.append(
                pltpu.make_async_remote_copy(
                    flow_v.at[:, pl.ds(h * 32 + 24, 8), :], halo_lo.at[:, h],
                    hs_sem.at[h], hr_sem.at[h], device_id={"pitch": up_p}, device_id_type=MESH,
                )
            )
            copies.append(
                pltpu.make_async_remote_copy(
                    flow_v.at[:, pl.ds(h * 32, 8), :], halo_hi.at[:, h],
                    hs_sem.at[2 + h], hr_sem.at[2 + h], device_id={"pitch": dn_p}, device_id_type=MESH,
                )
            )
        return copies

    for c in halos():
        c.start()

    def rotor_copies():
        return [
            pltpu.make_async_remote_copy(
                rots, rot.at[pt], gs_sem.at[d], gr_sem.at[d],
                device_id={"pitch": lax.rem(pt + d, NPI)}, device_id_type=MESH,
            )
            for d in range(1, NPI)
        ]

    @pl.when(is_cut)
    def _():
        rots[...] = flow_v[:, pl.ds(7, 4, stride=8), :]
        rot[pt] = flow_v[:, pl.ds(7, 4, stride=8), :]
        pltpu.make_async_copy(partner, part_s, ld_sem.at[6]).start()
        for c in rotor_copies():
            c.start()

    for c in loads[1:4]:
        c.wait()

    def block(ref, i):
        return ref[:, pl.ds(i, 8, stride=8), :].reshape(NC, NC, 8, 128)

    def first(i, f):
        s = mm(block(d_v, i), block(l_v, i))
        s_v[i] = s
        f = jnp.where(i == 0, s, mm(s, f))
        f_v[i] = f
        return f

    lax.fori_loop(0, 8, lambda i, _: (first(i, f_v[jnp.maximum(i - 1, 0)]), 0)[1], 0)

    def last(j, _):
        i = 7 - j
        n = jnp.minimum(i + 1, 7)
        t = mm(block(d_v, i), block(u_v, i))
        t_v[i] = t
        q_v[i] = jnp.where(i == 7, t, mm(t, q_v[n]))
        p_v[i] = f_v[i] + jnp.where(i == 7, 0.0, mm(t, p_v[n]))
        return 0

    lax.fori_loop(0, 8, last, 0)

    keep = jnp.where(is_cut, 0.0, 1.0)
    m0, m1 = f_v[7, :, :, 0:4, :], f_v[7, :, :, 4:8, :]
    m_d[...] = mm(m1, m0) * keep
    b0, b1 = q_v[0, :, :, 0:4, :], q_v[0, :, :, 4:8, :]
    b_d[...] = mm(b0, b1) * keep
    w0, w1 = p_v[0, :, :, 0:4, :], p_v[0, :, :, 4:8, :]
    w_d[...] = w0 + mm(b0, mm(w1, m0)) * keep

    for c in loads[4:]:
        c.wait()
    for c in halos():
        c.wait()

    for h in range(2):
        for c in range(4):
            r = h * 32 + c * 8
            mid = flow_v[:, r : r + 8, :]
            lo = halo_lo[:, h] if c == 0 else flow_v[:, r - 8 : r, :]
            hi = halo_hi[:, h] if c == 3 else flow_v[:, r + 8 : r + 16, :]
            src_v[:, r : r + 8, :] = res_v[:, r : r + 8, :] + spr_v[r : r + 8, :][None] * (
                hi + lo - 2.0 * mid
            )

    star = None
    for i in range(8):
        now = mv(block(d_v, i), src_v[:, pl.ds(i, 8, stride=8), :])
        star = now if star is None else now + mv(s_v[i], star)
        c_v[i] = star
    vh[0] = star
    ch = star
    for i in range(6, -1, -1):
        ch = c_v[i] + mv(t_v[i], ch)
        c_v[i] = ch
    vh[1] = ch
    v0, v1 = vh[0, :, 0:4, :], vh[0, :, 4:8, :]
    ww0, ww1 = vh[1, :, 0:4, :], vh[1, :, 4:8, :]
    ghost[...] = v0

    @pl.when(is_cut)
    def _():
        pltpu.make_async_copy(partner, part_s, ld_sem.at[6]).wait()
        for c in rotor_copies():
            c.wait()
        for k in range(4):
            who = part_s[pt * 4 + k]
            ghost[:, k : k + 1, :] = rot[who // 4, :, pl.ds(who % 4, 1), :]

    a1_base = ghost[...]
    v_d[...] = mv(m1, a1_base) + v1
    ww_d[...] = ww0 + mv(b0, mv(w1, v0) + ww1) * keep

    def f_copy(t):
        return pltpu.make_async_remote_copy(
            fsend.at[t], frecv.at[t], fs_sem.at[t], fr_sem.at[t],
            device_id={"stream": up_s}, device_id_type=MESH,
        )

    def b_copy(t):
        return pltpu.make_async_remote_copy(
            bsend.at[t], brecv.at[t], bs_sem.at[t], br_sem.at[t],
            device_id={"stream": dn_s}, device_id_type=MESH,
        )

    a_in = None
    first_keep = jnp.where(lax.rem(st, CUT) == 0, 0.0, 1.0)
    for t in range(HOPS):
        fsend[t] = v_d[...] if t == 0 else mv(m_d[...], a_in) * first_keep + v_d[...]
        f_copy(t).start()
        f_copy(t).wait_recv()
        a_in = frecv[t]
    a_in = a_in * jnp.where(st == 0, 0.0, 1.0)
    y = mv(w_d[...], a_in) + ww_d[...]
    b_in = None
    last_keep = jnp.where(st == NS - 1, 0.0, 1.0)
    for t in range(HOPS):
        bsend[t] = y if t == 0 else mv(b_d[...], b_in) * last_keep + y
        b_copy(t).start()
        b_copy(t).wait_recv()
        b_in = brecv[t]
    b_in = b_in * last_keep

    a1 = mv(m0, a_in) * keep + a1_base
    b_h0 = (mv(b1, b_in) + mv(w1, a1) + ww1) * keep
    vh[0, :, 0:4, :] = a_in
    vh[0, :, 4:8, :] = a1
    vh[1, :, 0:4, :] = b_h0
    vh[1, :, 4:8, :] = b_in
    a_h, b_h = vh[0], vh[1]
    for i in range(8):
        out[:, pl.ds(i, 8, stride=8), :] = (
            flow_v[:, pl.ds(i, 8, stride=8), :] + c_v[i] + mv(p_v[i], a_h) + mv(q_v[i], b_h)
        )
    for t in range(HOPS):
        f_copy(t).wait_send()
        b_copy(t).wait_send()


def to_tiles(x):
    lead = x.shape[:-2]
    x = x.reshape(lead + (2, 8, 4, 128))
    n = len(lead)
    x = jnp.transpose(x, tuple(range(n)) + (n, n + 2, n + 1, n + 3))
    return x.reshape(lead + (64, 128))


def from_tiles(x):
    lead = x.shape[:-2]
    x = x.reshape(lead + (2, 4, 8, 128))
    n = len(lead)
    x = jnp.transpose(x, tuple(range(n)) + (n, n + 2, n + 1, n + 3))
    return x.reshape(lead + (16, 512))


def local(flow_state, residual, spread, diag_inv, lower_jac, upper_jac, partner):
    f32 = jnp.float32
    vm = lambda *s: pltpu.VMEM(s, f32)
    dma = lambda n: pltpu.SemaphoreType.DMA((n,))
    hbm = pl.BlockSpec(memory_space=pltpu.HBM)
    updated = pl.pallas_call(
        kernel,
        out_shape=jax.ShapeDtypeStruct((NC, 64, 128), f32),
        in_specs=[hbm] * 7,
        out_specs=pl.BlockSpec(memory_space=pltpu.VMEM),
        scratch_shapes=[
            vm(5, 64, 128), vm(5, 64, 128), vm(64, 128), vm(25, 64, 128), vm(25, 64, 128), vm(25, 64, 128), vm(5, 64, 128),
            vm(8, 5, 5, 8, 128), vm(8, 5, 5, 8, 128), vm(8, 5, 5, 8, 128), vm(8, 5, 5, 8, 128), vm(8, 5, 5, 8, 128), vm(8, 5, 8, 128),
            vm(5, 2, 8, 128), vm(5, 2, 8, 128), vm(NPI, 5, 4, 128), vm(5, 4, 128), vm(5, 4, 128),
            vm(5, 5, 4, 128), vm(5, 5, 4, 128), vm(5, 5, 4, 128), vm(5, 4, 128), vm(5, 4, 128), vm(2, 5, 8, 128),
            vm(HOPS, 5, 4, 128), vm(HOPS, 5, 4, 128), vm(HOPS, 5, 4, 128), vm(HOPS, 5, 4, 128),
            pltpu.SMEM((128,), jnp.int32), dma(7), dma(4), dma(4), dma(NPI), dma(NPI), dma(HOPS), dma(HOPS), dma(HOPS), dma(HOPS),
        ],
        compiler_params=pltpu.CompilerParams(
            collective_id=0, has_side_effects=True, vmem_limit_bytes=60 * 1024 * 1024
        ),
        name="lusgs",
    )(
        to_tiles(flow_state), to_tiles(residual), to_tiles(spread), to_tiles(diag_inv),
        to_tiles(lower_jac), to_tiles(upper_jac), partner,
    )
    return from_tiles(updated)


def solution(mesh):
    blocks = P(None, "stream", "pitch")
    in_specs = (blocks, blocks, P("stream", "pitch"), blocks, blocks, blocks, P())
    return jax.shard_map(local, mesh=mesh, in_specs=in_specs, out_specs=blocks, check_vma=False)
```

time: 473 us -> 63.2 us (0.13)
  the two profiles are of different devices: /device:TPU:224 before, /device:TPU:32 now
where the time goes in v1:
time: 63.2 us; the launch traced here: 63.1 us
  Pallas kernels  61.5 us (97%)
  local copies, waits for them, and re-layouts  1.59 us (3%)
    pallas_call x1, Pallas kernels, local(): pl.pallas_call(kernel, out_shape=jax.ShapeDtypeStruct((NC, 64, 128), f32)...  61.5 us
    unnamed x1, local copies, waits for them, and re-layouts  1.59 us

profile of v1, /device:TPU:32, one launch (start us, length us, event | category | flops | bytes accessed | tf_op | source)
XLA Modules:
  0.0 63.1 jit_solution(13699975930120106875)
XLA Ops:
  0.0 61.5 %lusgs.1 = f32[5,64,128]{2,1,0:T(8,128)} custom-call(f32[5,64,128]{2,1,0:T(8,128)} %bitcast.39, f32[5,64,128]{2,1,0:T(8,128)} %bitcast.40, f32[64,128]{1,0:T(8,128)} %bitcast.41, f32[25,64,128]{2,1,0:T(8,128)} %bitcast.35, f32[25,64,128]{2,1,0:T(8,128)} %bitcast.36, f32[25,64,128]{2,1,0:T(8,128)} %bitcast.37, s32[128]{0:T(128)} %partner.1), custom_call_target="tpu_custom_call" | custom-call | tf_op jit(solution)/shard_map/lusgs/pallas_call | solution.py:245
  61.5 1.6 %copy.9 = f32[5,16,512]{2,1,0:T(8,128)} copy(f32[5,16,512]{2,1,0:T(8,128)} %bitcast.38) | data formatting | bytes 327680

commit v2 on v1

v2 whole, which is shorter than its diff:
```python
import jax
import jax.numpy as jnp
from jax import lax
from jax.experimental import pallas as pl
from jax.experimental.pallas import tpu as pltpu
from jax.sharding import PartitionSpec as P

MESH = pl.DeviceIdType.MESH
NC = 5
NS = 16
NPI = 32
CUT = 8
MID = 5


def mm(a, b):
    return jnp.stack([sum(a[r, k][None] * b[k] for k in range(NC)) for r in range(NC)])


def mv(a, x):
    return sum(a[:, k] * x[k][None] for k in range(NC))


def kernel(
    flow, res, spr, dinv, low, upp, partner, out,
    flow_v, res_v, spr_v, d_v, l_v, u_v, src_v,
    s_v, t_v, f_v, q_v, p_v, c_v,
    halo_lo, halo_hi, rot, rots, ghost,
    maps, vecs, vh, c_maps, c_vecs, answer, in_a, in_b, side_b, side_y, y_out,
    part_s, ld_sem, hs_sem, hr_sem, gs_sem, gr_sem,
    ms_sem, cm_sem, vs_sem, cv_sem, sbs_sem, sbr_sem, sys_sem, syr_sem, as_sem, ar_sem, bs_sem, br_sem,
):
    st = lax.axis_index("stream")
    pt = lax.axis_index("pitch")
    up_p, dn_p = lax.rem(pt + 1, NPI), lax.rem(pt + NPI - 1, NPI)
    is_cut = st == CUT
    pos = lax.rem(st, CUT)
    base = st - pos
    core = lax.rem(pt, 2)
    pair = pt - core
    centre = base + MID
    before = lax.rem(st + NS - CUT + MID, NS)
    is_mid = (pos == MID) & (core == 1)
    left = pos < MID

    def to(stream, pitch):
        return dict(device_id=(stream, pitch), device_id_type=MESH)

    loads = [
        pltpu.make_async_copy(h, v, ld_sem.at[i])
        for i, (h, v) in enumerate(
            ((flow, flow_v), (dinv, d_v), (low, l_v), (upp, u_v), (res, res_v), (spr, spr_v))
        )
    ]

    barrier = pltpu.get_barrier_semaphore()
    for nb in (up_p, dn_p):
        pl.semaphore_signal(barrier, inc=1, **to(st, nb))

    @pl.when(jnp.logical_not(is_mid))
    def _():
        pl.semaphore_signal(barrier, inc=1, **to(centre, pair + 1))

    @pl.when(pos == 0)
    def _():
        pl.semaphore_signal(barrier, inc=1, **to(before, pair + 1))

    @pl.when(left)
    def _():
        for q in range(MID):
            @pl.when(pos != q)
            def _():
                pl.semaphore_signal(barrier, inc=1, **to(base + q, pt))

    @pl.when(is_mid)
    def _():
        for q in range(CUT + 1):
            for k in range(2):
                if (q, k) != (MID, 1):
                    pl.semaphore_signal(barrier, inc=1, **to(lax.rem(base + q, NS), pair + k))

    @pl.when(is_cut)
    def _():
        for d in range(2, NPI - 1):
            pl.semaphore_signal(barrier, inc=1, **to(st, lax.rem(pt + d, NPI)))

    for c in loads:
        c.start()

    expected = (
        jnp.where(is_cut, NPI - 1, 2) + jnp.where(is_mid, 2 * CUT + 1, 1)
        + jnp.where(pos == 0, 1, 0) + jnp.where(left, MID - 1, 0)
    )
    pl.semaphore_wait(barrier, expected)

    loads[0].wait()

    def halos():
        copies = []
        for h in range(2):
            copies.append(
                pltpu.make_async_remote_copy(
                    flow_v.at[:, pl.ds(h * 32 + 24, 8), :], halo_lo.at[:, h],
                    hs_sem.at[h], hr_sem.at[h], **to(st, up_p),
                )
            )
            copies.append(
                pltpu.make_async_remote_copy(
                    flow_v.at[:, pl.ds(h * 32, 8), :], halo_hi.at[:, h],
                    hs_sem.at[2 + h], hr_sem.at[2 + h], **to(st, dn_p),
                )
            )
        return copies

    for c in halos():
        c.start()

    def rotor_copies():
        return [
            pltpu.make_async_remote_copy(
                rots, rot.at[pt], gs_sem.at[d], gr_sem.at[d], **to(st, lax.rem(pt + d, NPI))
            )
            for d in range(1, NPI)
        ]

    @pl.when(is_cut)
    def _():
        rots[...] = flow_v[:, pl.ds(7, 4, stride=8), :]
        rot[pt] = flow_v[:, pl.ds(7, 4, stride=8), :]
        pltpu.make_async_copy(partner, part_s, ld_sem.at[6]).start()
        for c in rotor_copies():
            c.start()

    for c in loads[1:4]:
        c.wait()

    def block(ref, i):
        return ref[:, pl.ds(i, 8, stride=8), :].reshape(NC, NC, 8, 128)

    def first(i, f):
        s = mm(block(d_v, i), block(l_v, i))
        s_v[i] = s
        f = jnp.where(i == 0, s, mm(s, f))
        f_v[i] = f
        return f

    lax.fori_loop(0, 8, lambda i, _: (first(i, f_v[jnp.maximum(i - 1, 0)]), 0)[1], 0)

    keep = jnp.where(is_cut, 0.0, 1.0)
    m0, m1 = f_v[7, :, :, 0:4, :], f_v[7, :, :, 4:8, :]
    maps[0] = mm(m1, m0)

    def map_copy(k, stream=centre):
        slot = pos
        return pltpu.make_async_remote_copy(
            maps.at[k], c_maps.at[core, slot, k], ms_sem.at[k], cm_sem.at[core, slot, k], **to(stream, pair + 1)
        )

    near = (pos >= MID) & jnp.logical_not(is_mid)

    @pl.when(((pos > 0) & left) | near)
    def _():
        map_copy(0).start()

    def last(j, _):
        i = 7 - j
        n = jnp.minimum(i + 1, 7)
        t = mm(block(d_v, i), block(u_v, i))
        t_v[i] = t
        q_v[i] = jnp.where(i == 7, t, mm(t, q_v[n]))
        p_v[i] = f_v[i] + jnp.where(i == 7, 0.0, mm(t, p_v[n]))
        return 0

    lax.fori_loop(0, 8, last, 0)

    b0, b1 = q_v[0, :, :, 0:4, :], q_v[0, :, :, 4:8, :]
    maps[1] = mm(b0, b1)
    w0, w1 = p_v[0, :, :, 0:4, :], p_v[0, :, :, 4:8, :]
    maps[2] = (w0 + mm(b0, mm(w1, m0)) * keep) * jnp.where(st == 0, 0.0, 1.0)

    def side_b_copy(q):
        return pltpu.make_async_remote_copy(
            maps.at[1], side_b.at[pos], sbs_sem.at[q], sbr_sem.at[pos], **to(base + q, pt)
        )

    @pl.when(near)
    def _():
        map_copy(1).start()
        map_copy(2).start()

    @pl.when(pos == 0)
    def _():
        map_copy(2, before).start()

    for q in range(MID - 1):
        @pl.when(left & (pos > q))
        def _():
            side_b_copy(q).start()

    for c in loads[4:]:
        c.wait()
    for c in halos():
        c.wait()

    for h in range(2):
        for c in range(4):
            r = h * 32 + c * 8
            mid = flow_v[:, r : r + 8, :]
            lo = halo_lo[:, h] if c == 0 else flow_v[:, r - 8 : r, :]
            hi = halo_hi[:, h] if c == 3 else flow_v[:, r + 8 : r + 16, :]
            src_v[:, r : r + 8, :] = res_v[:, r : r + 8, :] + spr_v[r : r + 8, :][None] * (
                hi + lo - 2.0 * mid
            )

    star = None
    for i in range(8):
        now = mv(block(d_v, i), src_v[:, pl.ds(i, 8, stride=8), :])
        star = now if star is None else now + mv(s_v[i], star)
        c_v[i] = star
    vh[0] = star
    v0, v1 = vh[0, :, 0:4, :], vh[0, :, 4:8, :]
    ghost[...] = v0

    def v_copy():
        return pltpu.make_async_remote_copy(
            vecs.at[0], c_vecs.at[core, pos, 0], vs_sem.at[0], cv_sem.at[core, pos, 0], **to(centre, pair + 1)
        )

    def w_copy(stream, slot):
        return pltpu.make_async_remote_copy(
            vecs.at[1], c_vecs.at[core, slot, 1], vs_sem.at[1], cv_sem.at[core, slot, 1], **to(stream, pair + 1)
        )

    @pl.when(jnp.logical_not(is_cut))
    def _():
        vecs[0] = mv(m1, v0) + v1

        @pl.when(jnp.logical_not(is_mid))
        def _():
            v_copy().start()

    ch = star
    for i in range(6, -1, -1):
        ch = c_v[i] + mv(t_v[i], ch)
        c_v[i] = ch
    vh[1] = ch
    ww0, ww1 = vh[1, :, 0:4, :], vh[1, :, 4:8, :]
    vecs[1] = (ww0 + mv(b0, mv(w1, v0) + ww1) * keep) * jnp.where(st == 0, 0.0, 1.0)

    @pl.when(near)
    def _():
        w_copy(centre, pos).start()

    @pl.when(pos == 0)
    def _():
        w_copy(before, 0).start()

    @pl.when(is_cut)
    def _():
        pltpu.make_async_copy(partner, part_s, ld_sem.at[6]).wait()
        for c in rotor_copies():
            c.wait()
        for k in range(4):
            who = part_s[pt * 4 + k]
            ghost[:, k : k + 1, :] = rot[who // 4, :, pl.ds(who % 4, 1), :]
        vecs[0] = mv(m1, ghost[...]) + v1
        v_copy().start()

    def a_copy(k, q):
        return pltpu.make_async_remote_copy(
            answer.at[0, k, q], in_a, as_sem.at[k, q], ar_sem.at[0], **to(lax.rem(base + q, NS), pair + k)
        )

    def b_copy(k, q):
        return pltpu.make_async_remote_copy(
            answer.at[1, k, max(q, MID - 1)], in_b, bs_sem.at[k, q], br_sem.at[0], **to(base + q, pair + k)
        )

    def arrived_map(k, q, m):
        pltpu.make_async_copy(maps.at[m], c_maps.at[k, q, m], cm_sem.at[k, q, m]).wait()

    def arrived_vec(k, q, m):
        pltpu.make_async_copy(vecs.at[m], c_vecs.at[k, q, m], cv_sem.at[k, q, m]).wait()

    a_sent = [(k, q) for q in range(1, CUT + 1) for k in range(2) if (k, q) != (1, MID)]
    b_sent = [(k, q) for q in range(CUT) for k in range(2) if (k, q) != (1, MID)]

    @pl.when(is_mid)
    def _():
        c_maps[1, MID] = maps[...]
        c_vecs[1, MID] = vecs[...]
        for k in range(2):
            for q in range(MID):
                if q:
                    arrived_map(k, q, 0)
                arrived_vec(k, q, 0)
        a = [c_vecs[0, 0, 0], c_vecs[1, 0, 0]]
        for q in range(1, MID + 1):
            for k in range(2):
                answer[0, k, q] = a[k]
                if q < MID:
                    a_copy(k, q).start()
                    a[k] = mv(c_maps[k, q, 0], a[k]) + c_vecs[k, q, 0]
        for k in range(2):
            for q in range(MID, CUT):
                if (k, q) != (1, MID):
                    for m in range(3):
                        arrived_map(k, q, m)
                    for m in range(2):
                        arrived_vec(k, q, m)
            arrived_map(k, 0, 2)
            arrived_vec(k, 0, 1)
        for q in range(MID, CUT):
            for k in range(2):
                a[k] = mv(c_maps[k, q, 0], a[k]) + c_vecs[k, q, 0]
                answer[0, k, q + 1] = a[k]
        b = [None, None]
        for k in range(2):
            b[k] = mv(c_maps[k, 0, 2], a[k]) + c_vecs[k, 0, 1]
            answer[1, k, CUT - 1] = b[k]
        for q in range(CUT - 1, MID - 1, -1):
            for k in range(2):
                b[k] = mv(c_maps[k, q, 1], b[k]) + mv(c_maps[k, q, 2], answer[0, k, q]) + c_vecs[k, q, 1]
                answer[1, k, q - 1] = b[k]
        for k, q in b_sent:
            b_copy(k, q).start()
        for k, q in a_sent:
            if q >= MID:
                a_copy(k, q).start()
        in_a[...] = answer[0, 1, MID]
        in_b[...] = answer[1, 1, MID]

    @pl.when(jnp.logical_not(is_mid))
    def _():
        a_copy(0, 1).wait_recv()

    a_in = in_a[...] * jnp.where(st == 0, 0.0, 1.0)

    def side_y_copy(q):
        return pltpu.make_async_remote_copy(
            y_out, side_y.at[pos], sys_sem.at[q], syr_sem.at[pos], **to(base + q, pt)
        )

    @pl.when(left & (pos > 0))
    def _():
        y_out[...] = mv(maps[2], a_in) + vecs[1]
        for q in range(MID - 1):
            @pl.when(pos > q)
            def _():
                side_y_copy(q).start()

    for e in range(1, MID):
        @pl.when(pos < e)
        def _():
            pltpu.make_async_copy(maps.at[1], side_b.at[e], sbr_sem.at[e]).wait()
            pltpu.make_async_copy(y_out, side_y.at[e], syr_sem.at[e]).wait()

    @pl.when(jnp.logical_not(is_mid))
    def _():
        b_copy(0, 0).wait_recv()

    for e in range(MID - 1, 0, -1):
        @pl.when(pos < e)
        def _():
            in_b[...] = mv(side_b[e], in_b[...]) + side_y[e]

    b_in = in_b[...] * jnp.where(st == NS - 1, 0.0, 1.0)

    a1 = jnp.where(is_cut, ghost[...], mv(m0, a_in) + v0)
    b_h0 = (mv(b1, b_in) + mv(w1, a1) + ww1) * keep
    vh[0, :, 0:4, :] = a_in
    vh[0, :, 4:8, :] = a1
    vh[1, :, 0:4, :] = b_h0
    vh[1, :, 4:8, :] = b_in
    a_h, b_h = vh[0], vh[1]
    for i in range(8):
        out[:, pl.ds(i, 8, stride=8), :] = (
            flow_v[:, pl.ds(i, 8, stride=8), :] + c_v[i] + mv(p_v[i], a_h) + mv(q_v[i], b_h)
        )

    @pl.when(((pos > 0) & left) | near)
    def _():
        map_copy(0).wait_send()

    @pl.when(near)
    def _():
        map_copy(1).wait_send()

    @pl.when(near | (pos == 0))
    def _():
        map_copy(2).wait_send()
        w_copy(centre, pos).wait_send()

    @pl.when(jnp.logical_not(is_mid))
    def _():
        v_copy().wait_send()

    for q in range(MID - 1):
        @pl.when(left & (pos > q))
        def _():
            side_b_copy(q).wait_send()
            side_y_copy(q).wait_send()

    @pl.when(is_mid)
    def _():
        for k, q in a_sent:
            a_copy(k, q).wait_send()
        for k, q in b_sent:
            b_copy(k, q).wait_send()


def to_tiles(x):
    lead = x.shape[:-2]
    x = x.reshape(lead + (2, 8, 4, 128))
    n = len(lead)
    x = jnp.transpose(x, tuple(range(n)) + (n, n + 2, n + 1, n + 3))
    return x.reshape(lead + (64, 128))


def from_tiles(x):
    lead = x.shape[:-2]
    x = x.reshape(lead + (2, 4, 8, 128))
    n = len(lead)
    x = jnp.transpose(x, tuple(range(n)) + (n, n + 2, n + 1, n + 3))
    return x.reshape(lead + (16, 512))


def local(flow_state, residual, spread, diag_inv, lower_jac, upper_jac, partner):
    f32 = jnp.float32
    vm = lambda *s: pltpu.VMEM(s, f32)
    dma = lambda *n: pltpu.SemaphoreType.DMA(n)
    hbm = pl.BlockSpec(memory_space=pltpu.HBM)
    updated = pl.pallas_call(
        kernel,
        out_shape=jax.ShapeDtypeStruct((NC, 64, 128), f32),
        in_specs=[hbm] * 7,
        out_specs=pl.BlockSpec(memory_space=pltpu.VMEM),
        scratch_shapes=[
            vm(5, 64, 128), vm(5, 64, 128), vm(64, 128), vm(25, 64, 128), vm(25, 64, 128), vm(25, 64, 128), vm(5, 64, 128),
            vm(8, 5, 5, 8, 128), vm(8, 5, 5, 8, 128), vm(8, 5, 5, 8, 128), vm(8, 5, 5, 8, 128), vm(8, 5, 5, 8, 128), vm(8, 5, 8, 128),
            vm(5, 2, 8, 128), vm(5, 2, 8, 128), vm(NPI, 5, 4, 128), vm(5, 4, 128), vm(5, 4, 128),
            vm(3, 5, 5, 4, 128), vm(2, 5, 4, 128), vm(2, 5, 8, 128),
            vm(2, CUT, 3, 5, 5, 4, 128), vm(2, CUT, 2, 5, 4, 128), vm(2, 2, CUT + 1, 5, 4, 128),
            vm(5, 4, 128), vm(5, 4, 128), vm(MID, 5, 5, 4, 128), vm(MID, 5, 4, 128), vm(5, 4, 128),
            pltpu.SMEM((128,), jnp.int32), dma(7), dma(4), dma(4), dma(NPI), dma(NPI),
            dma(3), dma(2, CUT, 3), dma(2), dma(2, CUT, 2), dma(MID), dma(MID), dma(MID), dma(MID),
            dma(2, CUT + 1), dma(1), dma(2, CUT + 1), dma(1),
        ],
        compiler_params=pltpu.CompilerParams(
            collective_id=0, has_side_effects=True, vmem_limit_bytes=60 * 1024 * 1024
        ),
        name="lusgs",
    )(
        to_tiles(flow_state), to_tiles(residual), to_tiles(spread), to_tiles(diag_inv),
        to_tiles(lower_jac), to_tiles(upper_jac), partner,
    )
    return from_tiles(updated)


def solution(mesh):
    blocks = P(None, "stream", "pitch")
    in_specs = (blocks, blocks, P("stream", "pitch"), blocks, blocks, blocks, P())
    return jax.shard_map(local, mesh=mesh, in_specs=in_specs, out_specs=blocks, check_vma=False)
```

time: 63.2 us -> 36.5 us (0.58)
  the two profiles are of different devices: /device:TPU:32 before, /device:TPU:1 now
where the time goes in v2:
time: 36.5 us; the launch traced here: 36.4 us
  Pallas kernels  34.8 us (95%)
  local copies, waits for them, and re-layouts  1.59 us (4%)
    pallas_call x1, Pallas kernels, local(): pl.pallas_call(kernel, out_shape=jax.ShapeDtypeStruct((NC, 64, 128), f32)...  34.8 us
    unnamed x1, local copies, waits for them, and re-layouts  1.59 us

profile of v2, /device:TPU:1, one launch (start us, length us, event | category | flops | bytes accessed | tf_op | source)
XLA Modules:
  0.0 36.4 jit_solution(2203287444120759606)
XLA Ops:
  0.0 34.8 %lusgs.1 = f32[5,64,128]{2,1,0:T(8,128)} custom-call(f32[5,64,128]{2,1,0:T(8,128)} %bitcast.39, f32[5,64,128]{2,1,0:T(8,128)} %bitcast.40, f32[64,128]{1,0:T(8,128)} %bitcast.41, f32[25,64,128]{2,1,0:T(8,128)} %bitcast.35, f32[25,64,128]{2,1,0:T(8,128)} %bitcast.36, f32[25,64,128]{2,1,0:T(8,128)} %bitcast.37, s32[128]{0:T(128)} %partner.1), custom_call_target="tpu_custom_call" | custom-call | tf_op jit(solution)/shard_map/lusgs/pallas_call | solution.py:433
  34.8 1.6 %copy.9 = f32[5,16,512]{2,1,0:T(8,128)} copy(f32[5,16,512]{2,1,0:T(8,128)} %bitcast.38) | data formatting | bytes 327680

commit v3 on v2

--- a/solution.py
+++ b/solution.py
@@ -10,6 +10,7 @@
 NS = 16
 NPI = 32
 CUT = 8
+ROW = 8
 MID = 5
 
 
@@ -25,9 +26,9 @@
     flow, res, spr, dinv, low, upp, partner, out,
     flow_v, res_v, spr_v, d_v, l_v, u_v, src_v,
     s_v, t_v, f_v, q_v, p_v, c_v,
-    halo_lo, halo_hi, rot, rots, ghost,
+    halo_lo, halo_hi, rot, rots, chosen, facing, ghost,
     maps, vecs, vh, c_maps, c_vecs, answer, in_a, in_b, side_b, side_y, y_out,
-    part_s, ld_sem, hs_sem, hr_sem, gs_sem, gr_sem,
+    part_s, ld_sem, hs_sem, hr_sem, gs_sem, gr_sem, xs_sem, xr_sem, ready,
     ms_sem, cm_sem, vs_sem, cv_sem, sbs_sem, sbr_sem, sys_sem, syr_sem, as_sem, ar_sem, bs_sem, br_sem,
 ):
     st = lax.axis_index("stream")
@@ -42,6 +43,10 @@
     before = lax.rem(st + NS - CUT + MID, NS)
     is_mid = (pos == MID) & (core == 1)
     left = pos < MID
+    near = (pos >= MID) & jnp.logical_not(is_mid)
+    row = pt // ROW
+    row_peers = [row * ROW + lax.rem(pt + d, ROW) for d in range(1, ROW)]
+    column_peers = [lax.rem(pt + d * ROW, NPI) for d in range(1, NPI // ROW)]
 
     def to(stream, pitch):
         return dict(device_id=(stream, pitch), device_id_type=MESH)
@@ -53,45 +58,50 @@
         )
     ]
 
+    loads[0].start()
     barrier = pltpu.get_barrier_semaphore()
     for nb in (up_p, dn_p):
         pl.semaphore_signal(barrier, inc=1, **to(st, nb))
 
-    @pl.when(jnp.logical_not(is_mid))
+    @pl.when(left)
     def _():
         pl.semaphore_signal(barrier, inc=1, **to(centre, pair + 1))
-
-    @pl.when(pos == 0)
-    def _():
-        pl.semaphore_signal(barrier, inc=1, **to(before, pair + 1))
-
-    @pl.when(left)
-    def _():
-        for q in range(MID):
-            @pl.when(pos != q)
+        for q in range(1, MID):
+            @pl.when(pos < q)
             def _():
                 pl.semaphore_signal(barrier, inc=1, **to(base + q, pt))
 
     @pl.when(is_mid)
     def _():
-        for q in range(CUT + 1):
+        for q in range(MID, CUT):
             for k in range(2):
                 if (q, k) != (MID, 1):
-                    pl.semaphore_signal(barrier, inc=1, **to(lax.rem(base + q, NS), pair + k))
+                    pl.semaphore_signal(barrier, inc=1, **to(base + q, pair + k))
+
+        @pl.when(base == 0)
+        def _():
+            for k in range(2):
+                pl.semaphore_signal(barrier, inc=1, **to(CUT, pair + k))
 
     @pl.when(is_cut)
     def _():
-        for d in range(2, NPI - 1):
-            pl.semaphore_signal(barrier, inc=1, **to(st, lax.rem(pt + d, NPI)))
-
-    for c in loads:
+        for nb in row_peers + column_peers:
+            pl.semaphore_signal(barrier, inc=1, **to(st, nb))
+
+    for c in loads[1:]:
         c.start()
 
     expected = (
-        jnp.where(is_cut, NPI - 1, 2) + jnp.where(is_mid, 2 * CUT + 1, 1)
-        + jnp.where(pos == 0, 1, 0) + jnp.where(left, MID - 1, 0)
+        2 + jnp.where(is_cut, len(row_peers) + len(column_peers) + 1, 0) + jnp.where(is_mid, 2 * MID, 0)
+        + jnp.where(near, 1, 0) + jnp.where(left, pos, 0)
     )
     pl.semaphore_wait(barrier, expected)
+
+    @pl.when(is_mid)
+    def _():
+        for q in range(MID):
+            for k in range(2):
+                pl.semaphore_signal(ready, inc=1, **to(base + q, pair + k))
 
     loads[0].wait()
 
@@ -115,20 +125,33 @@
     for c in halos():
         c.start()
 
-    def rotor_copies():
+    def row_copies():
         return [
             pltpu.make_async_remote_copy(
-                rots, rot.at[pt], gs_sem.at[d], gr_sem.at[d], **to(st, lax.rem(pt + d, NPI))
+                rots, rot.at[lax.rem(pt, ROW)], gs_sem.at[d], gr_sem.at[d], **to(st, nb)
             )
-            for d in range(1, NPI)
+            for d, nb in enumerate(row_peers)
         ]
 
+    def column_copies():
+        return [
+            pltpu.make_async_remote_copy(
+                chosen.at[d], facing.at[row], xs_sem.at[d], xr_sem.at[d], **to(st, nb)
+            )
+            for d, nb in enumerate(column_peers)
+        ]
+
+    def choose(target, nb):
+        for k in range(4):
+            who = part_s[nb * 4 + k]
+            target[:, k : k + 1, :] = rot[lax.rem(who // 4, ROW), :, pl.ds(lax.rem(who, 4), 1), :]
+
     @pl.when(is_cut)
     def _():
         rots[...] = flow_v[:, pl.ds(7, 4, stride=8), :]
-        rot[pt] = flow_v[:, pl.ds(7, 4, stride=8), :]
+        rot[lax.rem(pt, ROW)] = flow_v[:, pl.ds(7, 4, stride=8), :]
         pltpu.make_async_copy(partner, part_s, ld_sem.at[6]).start()
-        for c in rotor_copies():
+        for c in row_copies():
             c.start()
 
     for c in loads[1:4]:
@@ -156,9 +179,7 @@
             maps.at[k], c_maps.at[core, slot, k], ms_sem.at[k], cm_sem.at[core, slot, k], **to(stream, pair + 1)
         )
 
-    near = (pos >= MID) & jnp.logical_not(is_mid)
-
-    @pl.when(((pos > 0) & left) | near)
+    @pl.when(near)
     def _():
         map_copy(0).start()
 
@@ -176,7 +197,7 @@
     b0, b1 = q_v[0, :, :, 0:4, :], q_v[0, :, :, 4:8, :]
     maps[1] = mm(b0, b1)
     w0, w1 = p_v[0, :, :, 0:4, :], p_v[0, :, :, 4:8, :]
-    maps[2] = (w0 + mm(b0, mm(w1, m0)) * keep) * jnp.where(st == 0, 0.0, 1.0)
+    maps[2] = w0 + mm(b0, mm(w1, m0)) * keep
 
     def side_b_copy(q):
         return pltpu.make_async_remote_copy(
@@ -188,7 +209,7 @@
         map_copy(1).start()
         map_copy(2).start()
 
-    @pl.when(pos == 0)
+    @pl.when(is_cut)
     def _():
         map_copy(2, before).start()
 
@@ -235,7 +256,7 @@
     def _():
         vecs[0] = mv(m1, v0) + v1
 
-        @pl.when(jnp.logical_not(is_mid))
+        @pl.when(near)
         def _():
             v_copy().start()
 
@@ -245,25 +266,44 @@
         c_v[i] = ch
     vh[1] = ch
     ww0, ww1 = vh[1, :, 0:4, :], vh[1, :, 4:8, :]
-    vecs[1] = (ww0 + mv(b0, mv(w1, v0) + ww1) * keep) * jnp.where(st == 0, 0.0, 1.0)
+    vecs[1] = ww0 + mv(b0, mv(w1, v0) + ww1) * keep
 
     @pl.when(near)
     def _():
         w_copy(centre, pos).start()
 
-    @pl.when(pos == 0)
+    @pl.when(is_cut)
     def _():
         w_copy(before, 0).start()
 
+    @pl.when(left & jnp.logical_not(is_cut))
+    def _():
+        pl.semaphore_wait(ready, 1)
+        v_copy().start()
+
+        @pl.when(pos > 0)
+        def _():
+            map_copy(0).start()
+
     @pl.when(is_cut)
     def _():
         pltpu.make_async_copy(partner, part_s, ld_sem.at[6]).wait()
-        for c in rotor_copies():
+        for c in row_copies():
+            c.wait()
+        choose(facing.at[row], pt)
+        for d, c in enumerate(column_copies()):
+            choose(chosen.at[d], column_peers[d])
+            c.start()
+
+    @pl.when(is_cut)
+    def _():
+        for c in column_copies():
             c.wait()
         for k in range(4):
             who = part_s[pt * 4 + k]
-            ghost[:, k : k + 1, :] = rot[who // 4, :, pl.ds(who % 4, 1), :]
+            ghost[:, k : k + 1, :] = facing[who // (4 * ROW), :, pl.ds(k, 1), :]
         vecs[0] = mv(m1, ghost[...]) + v1
+        pl.semaphore_wait(ready, 1)
         v_copy().start()
 
     def a_copy(k, q):
@@ -308,33 +348,69 @@
                         arrived_map(k, q, m)
                     for m in range(2):
                         arrived_vec(k, q, m)
-            arrived_map(k, 0, 2)
-            arrived_vec(k, 0, 1)
+
+        @pl.when(base == 0)
+        def _():
+            for k in range(2):
+                arrived_map(k, 0, 2)
+
+        @pl.when(base != 0)
+        def _():
+            for k in range(2):
+                c_maps[k, 0, 2] = jnp.zeros((NC, NC, 4, 128), jnp.float32)
+                c_vecs[k, 0, 1] = jnp.zeros((NC, 4, 128), jnp.float32)
+
         for q in range(MID, CUT):
             for k in range(2):
                 a[k] = mv(c_maps[k, q, 0], a[k]) + c_vecs[k, q, 0]
                 answer[0, k, q + 1] = a[k]
-        b = [None, None]
+        b, g = [None, None], [None, None]
         for k in range(2):
-            b[k] = mv(c_maps[k, 0, 2], a[k]) + c_vecs[k, 0, 1]
+            b[k] = mv(c_maps[k, 0, 2], a[k])
             answer[1, k, CUT - 1] = b[k]
         for q in range(CUT - 1, MID - 1, -1):
             for k in range(2):
                 b[k] = mv(c_maps[k, q, 1], b[k]) + mv(c_maps[k, q, 2], answer[0, k, q]) + c_vecs[k, q, 1]
                 answer[1, k, q - 1] = b[k]
+                c_maps[k, q - MID, 1] = c_maps[k, q, 1] if q == CUT - 1 else mm(c_maps[k, q, 1], c_maps[k, q + 1 - MID, 1])
+
+        @pl.when(base == 0)
+        def _():
+            for k in range(2):
+                arrived_vec(k, 0, 1)
+
+        for q in range(MID - 1, CUT):
+            for k in range(2):
+                w = c_vecs[k, 0, 1]
+                answer[1, k, q] = answer[1, k, q] + (w if q == CUT - 1 else mv(c_maps[k, q + 1 - MID, 1], w))
+            if q == MID - 1:
+                for kk, qq in b_sent:
+                    if qq < MID:
+                        b_copy(kk, qq).start()
         for k, q in b_sent:
-            b_copy(k, q).start()
+            if q >= MID:
+                b_copy(k, q).start()
         for k, q in a_sent:
-            if q >= MID:
+            if MID <= q < CUT:
                 a_copy(k, q).start()
+
+        @pl.when(base == 0)
+        def _():
+            for k in range(2):
+                a_copy(k, CUT).start()
+
         in_a[...] = answer[0, 1, MID]
         in_b[...] = answer[1, 1, MID]
 
-    @pl.when(jnp.logical_not(is_mid))
+    @pl.when(jnp.logical_not(is_mid) & (st != 0))
     def _():
         a_copy(0, 1).wait_recv()
 
-    a_in = in_a[...] * jnp.where(st == 0, 0.0, 1.0)
+    @pl.when(st == 0)
+    def _():
+        in_a[...] = jnp.zeros((NC, 4, 128), jnp.float32)
+
+    a_in = in_a[...]
 
     def side_y_copy(q):
         return pltpu.make_async_remote_copy(
@@ -386,7 +462,7 @@
     def _():
         map_copy(1).wait_send()
 
-    @pl.when(near | (pos == 0))
+    @pl.when(near | is_cut)
     def _():
         map_copy(2).wait_send()
         w_copy(centre, pos).wait_send()
@@ -404,7 +480,14 @@
     @pl.when(is_mid)
     def _():
         for k, q in a_sent:
-            a_copy(k, q).wait_send()
+            if q < CUT:
+                a_copy(k, q).wait_send()
+
+        @pl.when(base == 0)
+        def _():
+            for k in range(2):
+                a_copy(k, CUT).wait_send()
+
         for k, q in b_sent:
             b_copy(k, q).wait_send()
 
@@ -438,11 +521,11 @@
         scratch_shapes=[
             vm(5, 64, 128), vm(5, 64, 128), vm(64, 128), vm(25, 64, 128), vm(25, 64, 128), vm(25, 64, 128), vm(5, 64, 128),
             vm(8, 5, 5, 8, 128), vm(8, 5, 5, 8, 128), vm(8, 5, 5, 8, 128), vm(8, 5, 5, 8, 128), vm(8, 5, 5, 8, 128), vm(8, 5, 8, 128),
-            vm(5, 2, 8, 128), vm(5, 2, 8, 128), vm(NPI, 5, 4, 128), vm(5, 4, 128), vm(5, 4, 128),
+            vm(5, 2, 8, 128), vm(5, 2, 8, 128), vm(ROW, 5, 4, 128), vm(5, 4, 128), vm(3, 5, 4, 128), vm(4, 5, 4, 128), vm(5, 4, 128),
             vm(3, 5, 5, 4, 128), vm(2, 5, 4, 128), vm(2, 5, 8, 128),
             vm(2, CUT, 3, 5, 5, 4, 128), vm(2, CUT, 2, 5, 4, 128), vm(2, 2, CUT + 1, 5, 4, 128),
             vm(5, 4, 128), vm(5, 4, 128), vm(MID, 5, 5, 4, 128), vm(MID, 5, 4, 128), vm(5, 4, 128),
-            pltpu.SMEM((128,), jnp.int32), dma(7), dma(4), dma(4), dma(NPI), dma(NPI),
+            pltpu.SMEM((128,), jnp.int32), dma(7), dma(4), dma(4), dma(ROW), dma(ROW), dma(3), dma(3), pltpu.SemaphoreType.REGULAR,
             dma(3), dma(2, CUT, 3), dma(2), dma(2, CUT, 2), dma(MID), dma(MID), dma(MID), dma(MID),
             dma(2, CUT + 1), dma(1), dma(2, CUT + 1), dma(1),
         ],

time: 36.5 us -> 31.5 us (0.86)
  Pallas kernels: 34.8 us -> 29.7 us
    pallas_call x1, Pallas kernels: 34.8 us -> 29.7 us  [local(): pl.pallas_call(kernel, out_shape=jax.ShapeDtypeStruct((NC, 64, 128), f32)...]
where the time goes in v3:
time: 31.5 us; the launch traced here: 31.3 us
  Pallas kernels  29.7 us (94%)
  local copies, waits for them, and re-layouts  1.59 us (5%)
    pallas_call x1, Pallas kernels, local(): pl.pallas_call(kernel, out_shape=jax.ShapeDtypeStruct((NC, 64, 128), f32)...  29.7 us
    unnamed x1, local copies, waits for them, and re-layouts  1.59 us

profile of v3, /device:TPU:1, one launch (start us, length us, event | category | flops | bytes accessed | tf_op | source)
XLA Modules:
  0.0 31.3 jit_solution(12435767021334615015)
XLA Ops:
  0.0 29.7 %lusgs.1 = f32[5,64,128]{2,1,0:T(8,128)} custom-call(f32[5,64,128]{2,1,0:T(8,128)} %bitcast.39, f32[5,64,128]{2,1,0:T(8,128)} %bitcast.40, f32[64,128]{1,0:T(8,128)} %bitcast.41, f32[25,64,128]{2,1,0:T(8,128)} %bitcast.35, f32[25,64,128]{2,1,0:T(8,128)} %bitcast.36, f32[25,64,128]{2,1,0:T(8,128)} %bitcast.37, s32[128]{0:T(128)} %partner.1), custom_call_target="tpu_custom_call" | custom-call | tf_op jit(solution)/shard_map/lusgs/pallas_call | solution.py:516
  29.7 1.6 %copy.9 = f32[5,16,512]{2,1,0:T(8,128)} copy(f32[5,16,512]{2,1,0:T(8,128)} %bitcast.38) | data formatting | bytes 327680

commit v4 on v3

--- a/solution.py
+++ b/solution.py
@@ -11,7 +11,9 @@
 NPI = 32
 CUT = 8
 ROW = 8
-MID = 5
+MID = 6
+LEFT = 5
+SUB = 3
 
 
 def mm(a, b):
@@ -27,9 +29,9 @@
     flow_v, res_v, spr_v, d_v, l_v, u_v, src_v,
     s_v, t_v, f_v, q_v, p_v, c_v,
     halo_lo, halo_hi, rot, rots, chosen, facing, ghost,
-    maps, vecs, vh, c_maps, c_vecs, answer, in_a, in_b, side_b, side_y, y_out,
+    maps, vecs, vh, c_maps, c_vecs, answer, in_a, in_b, side_b, side_y, y_out, hop_in,
     part_s, ld_sem, hs_sem, hr_sem, gs_sem, gr_sem, xs_sem, xr_sem, ready,
-    ms_sem, cm_sem, vs_sem, cv_sem, sbs_sem, sbr_sem, sys_sem, syr_sem, as_sem, ar_sem, bs_sem, br_sem,
+    ms_sem, cm_sem, vs_sem, cv_sem, sbs_sem, sbr_sem, sys_sem, syr_sem, as_sem, ar_sem, bs_sem, br_sem, hs2_sem, hr2_sem,
 ):
     st = lax.axis_index("stream")
     pt = lax.axis_index("pitch")
@@ -42,8 +44,12 @@
     centre = base + MID
     before = lax.rem(st + NS - CUT + MID, NS)
     is_mid = (pos == MID) & (core == 1)
-    left = pos < MID
-    near = (pos >= MID) & jnp.logical_not(is_mid)
+    left = pos < LEFT
+    chained = (base == 0) & (pos <= SUB)
+    is_sub = (base == 0) & (pos == SUB) & (core == 1)
+    home = jnp.where(chained, base + SUB, centre)
+    unheard = (base == 0) & (pt == 0)
+    near = (pos >= LEFT) & jnp.logical_not(is_mid)
     row = pt // ROW
     row_peers = [row * ROW + lax.rem(pt + d, ROW) for d in range(1, ROW)]
     column_peers = [lax.rem(pt + d * ROW, NPI) for d in range(1, NPI // ROW)]
@@ -65,15 +71,29 @@
 
     @pl.when(left)
     def _():
-        pl.semaphore_signal(barrier, inc=1, **to(centre, pair + 1))
-        for q in range(1, MID):
-            @pl.when(pos < q)
+        @pl.when((base != 0) | (pos >= SUB))
+        def _():
+            pl.semaphore_signal(barrier, inc=1, **to(centre, pair + 1))
+
+        for q in range(1, LEFT):
+            @pl.when((pos < q) & jnp.logical_not(unheard & (pos == 0)))
             def _():
                 pl.semaphore_signal(barrier, inc=1, **to(base + q, pt))
 
+    @pl.when((base == 0) & (pos == LEFT - 1))
+    def _():
+        pl.semaphore_signal(barrier, inc=1, **to(base + SUB, pair + 1))
+
+    @pl.when(is_sub)
+    def _():
+        for q in range(SUB + 1):
+            for k in range(2):
+                if (k, q) != (1, SUB):
+                    pl.semaphore_signal(barrier, inc=1, **to(base + q, pair + k))
+
     @pl.when(is_mid)
     def _():
-        for q in range(MID, CUT):
+        for q in range(LEFT, CUT):
             for k in range(2):
                 if (q, k) != (MID, 1):
                     pl.semaphore_signal(barrier, inc=1, **to(base + q, pair + k))
@@ -92,16 +112,19 @@
         c.start()
 
     expected = (
-        2 + jnp.where(is_cut, len(row_peers) + len(column_peers) + 1, 0) + jnp.where(is_mid, 2 * MID, 0)
-        + jnp.where(near, 1, 0) + jnp.where(left, pos, 0)
+        2 + jnp.where(is_cut, len(row_peers) + len(column_peers) + 1, 0) + jnp.where(is_mid, jnp.where(base == 0, 2 * (LEFT - SUB), 2 * LEFT), 0)
+        + jnp.where(near | (chained & jnp.logical_not(is_sub)), 1, 0) + jnp.where(is_sub, 2, 0)
+        + jnp.where(left & (pos > 0), pos - jnp.where(unheard, 1, 0), 0)
     )
     pl.semaphore_wait(barrier, expected)
 
     @pl.when(is_mid)
     def _():
-        for q in range(MID):
+        for q in range(LEFT):
             for k in range(2):
-                pl.semaphore_signal(ready, inc=1, **to(base + q, pair + k))
+                @pl.when((base != 0) | (q == LEFT - 1) | ((q == SUB) & (k == 1)))
+                def _():
+                    pl.semaphore_signal(ready, inc=1, **to(base + q, pair + k))
 
     loads[0].wait()
 
@@ -173,13 +196,13 @@
     m0, m1 = f_v[7, :, :, 0:4, :], f_v[7, :, :, 4:8, :]
     maps[0] = mm(m1, m0)
 
-    def map_copy(k, stream=centre):
+    def map_copy(k, stream=home):
         slot = pos
         return pltpu.make_async_remote_copy(
             maps.at[k], c_maps.at[core, slot, k], ms_sem.at[k], cm_sem.at[core, slot, k], **to(stream, pair + 1)
         )
 
-    @pl.when(near)
+    @pl.when(near | (chained & jnp.logical_not(is_sub) & (pos > 0)))
     def _():
         map_copy(0).start()
 
@@ -213,8 +236,8 @@
     def _():
         map_copy(2, before).start()
 
-    for q in range(MID - 1):
-        @pl.when(left & (pos > q))
+    for q in range(LEFT - 1):
+        @pl.when(left & (pos > q) & ((q > 0) | jnp.logical_not(unheard)))
         def _():
             side_b_copy(q).start()
 
@@ -244,7 +267,7 @@
 
     def v_copy():
         return pltpu.make_async_remote_copy(
-            vecs.at[0], c_vecs.at[core, pos, 0], vs_sem.at[0], cv_sem.at[core, pos, 0], **to(centre, pair + 1)
+            vecs.at[0], c_vecs.at[core, pos, 0], vs_sem.at[0], cv_sem.at[core, pos, 0], **to(home, pair + 1)
         )
 
     def w_copy(stream, slot):
@@ -276,12 +299,15 @@
     def _():
         w_copy(before, 0).start()
 
-    @pl.when(left & jnp.logical_not(is_cut))
-    def _():
-        pl.semaphore_wait(ready, 1)
+    @pl.when(left & jnp.logical_not(is_cut) & jnp.logical_not(is_sub))
+    def _():
+        @pl.when(jnp.logical_not(chained))
+        def _():
+            pl.semaphore_wait(ready, 1)
+
         v_copy().start()
 
-        @pl.when(pos > 0)
+        @pl.when((pos > 0) & jnp.logical_not(chained))
         def _():
             map_copy(0).start()
 
@@ -313,7 +339,7 @@
 
     def b_copy(k, q):
         return pltpu.make_async_remote_copy(
-            answer.at[1, k, max(q, MID - 1)], in_b, bs_sem.at[k, q], br_sem.at[0], **to(base + q, pair + k)
+            answer.at[1, k, max(q, LEFT - 1)], in_b, bs_sem.at[k, q], br_sem.at[0], **to(base + q, pair + k)
         )
 
     def arrived_map(k, q, m):
@@ -322,87 +348,115 @@
     def arrived_vec(k, q, m):
         pltpu.make_async_copy(vecs.at[m], c_vecs.at[k, q, m], cv_sem.at[k, q, m]).wait()
 
+    def hop_copy(k):
+        return pltpu.make_async_remote_copy(
+            answer.at[0, k, SUB + 1], hop_in.at[k], hs2_sem.at[k], hr2_sem.at[k], **to(centre, pt)
+        )
+
     a_sent = [(k, q) for q in range(1, CUT + 1) for k in range(2) if (k, q) != (1, MID)]
     b_sent = [(k, q) for q in range(CUT) for k in range(2) if (k, q) != (1, MID)]
 
+    @pl.when(is_sub)
+    def _():
+        c_maps[1, SUB, 0] = maps[0]
+        c_vecs[1, SUB, 0] = vecs[0]
+        for k in (1, 0):
+            for q in range(SUB + 1):
+                if (k, q) != (1, SUB):
+                    if q:
+                        arrived_map(k, q, 0)
+                    arrived_vec(k, q, 0)
+            hop = c_vecs[k, 0, 0]
+            for q in range(1, SUB + 2):
+                answer[0, k, q] = hop
+                if q <= SUB:
+                    hop = mv(c_maps[k, q, 0], hop) + c_vecs[k, q, 0]
+            for q in range(SUB + 1, 0, -1):
+                if (k, q) != (1, SUB):
+                    a_copy(k, q).start()
+            if k == 1:
+                in_a[...] = answer[0, 1, SUB]
+                pl.semaphore_wait(ready, 1)
+            hop_copy(k).start()
+
     @pl.when(is_mid)
     def _():
         c_maps[1, MID] = maps[...]
         c_vecs[1, MID] = vecs[...]
-        for k in range(2):
-            for q in range(MID):
-                if q:
-                    arrived_map(k, q, 0)
-                arrived_vec(k, q, 0)
-        a = [c_vecs[0, 0, 0], c_vecs[1, 0, 0]]
-        for q in range(1, MID + 1):
-            for k in range(2):
-                answer[0, k, q] = a[k]
-                if q < MID:
+        for k in (1, 0):
+            @pl.when(base == 0)
+            def _():
+                hop_copy(k).wait_recv()
+                answer[0, k, LEFT - 1] = hop_in[k]
+
+            @pl.when(base != 0)
+            def _():
+                for q in range(LEFT - 1):
+                    if q:
+                        arrived_map(k, q, 0)
+                    arrived_vec(k, q, 0)
+                early = c_vecs[k, 0, 0]
+                for q in range(1, LEFT):
+                    answer[0, k, q] = early
                     a_copy(k, q).start()
-                    a[k] = mv(c_maps[k, q, 0], a[k]) + c_vecs[k, q, 0]
-        for k in range(2):
-            for q in range(MID, CUT):
+                    if q < LEFT - 1:
+                        early = mv(c_maps[k, q, 0], early) + c_vecs[k, q, 0]
+
+            arrived_map(k, LEFT - 1, 0)
+            arrived_vec(k, LEFT - 1, 0)
+            a = mv(c_maps[k, LEFT - 1, 0], answer[0, k, LEFT - 1]) + c_vecs[k, LEFT - 1, 0]
+            answer[0, k, LEFT] = a
+            for q in range(LEFT, CUT):
                 if (k, q) != (1, MID):
                     for m in range(3):
                         arrived_map(k, q, m)
                     for m in range(2):
                         arrived_vec(k, q, m)
 
-        @pl.when(base == 0)
-        def _():
-            for k in range(2):
+            @pl.when(base == 0)
+            def _():
                 arrived_map(k, 0, 2)
 
-        @pl.when(base != 0)
-        def _():
-            for k in range(2):
+            @pl.when(base != 0)
+            def _():
                 c_maps[k, 0, 2] = jnp.zeros((NC, NC, 4, 128), jnp.float32)
                 c_vecs[k, 0, 1] = jnp.zeros((NC, 4, 128), jnp.float32)
 
-        for q in range(MID, CUT):
-            for k in range(2):
-                a[k] = mv(c_maps[k, q, 0], a[k]) + c_vecs[k, q, 0]
-                answer[0, k, q + 1] = a[k]
-        b, g = [None, None], [None, None]
-        for k in range(2):
-            b[k] = mv(c_maps[k, 0, 2], a[k])
-            answer[1, k, CUT - 1] = b[k]
-        for q in range(CUT - 1, MID - 1, -1):
-            for k in range(2):
-                b[k] = mv(c_maps[k, q, 1], b[k]) + mv(c_maps[k, q, 2], answer[0, k, q]) + c_vecs[k, q, 1]
-                answer[1, k, q - 1] = b[k]
-                c_maps[k, q - MID, 1] = c_maps[k, q, 1] if q == CUT - 1 else mm(c_maps[k, q, 1], c_maps[k, q + 1 - MID, 1])
-
-        @pl.when(base == 0)
-        def _():
-            for k in range(2):
+            for q in range(LEFT, CUT):
+                a = mv(c_maps[k, q, 0], a) + c_vecs[k, q, 0]
+                answer[0, k, q + 1] = a
+            b = mv(c_maps[k, 0, 2], a)
+            answer[1, k, CUT - 1] = b
+            for q in range(CUT - 1, LEFT - 1, -1):
+                b = mv(c_maps[k, q, 1], b) + mv(c_maps[k, q, 2], answer[0, k, q]) + c_vecs[k, q, 1]
+                answer[1, k, q - 1] = b
+                c_maps[k, q - LEFT, 1] = c_maps[k, q, 1] if q == CUT - 1 else mm(c_maps[k, q, 1], c_maps[k, q + 1 - LEFT, 1])
+
+            @pl.when(base == 0)
+            def _():
                 arrived_vec(k, 0, 1)
 
-        for q in range(MID - 1, CUT):
-            for k in range(2):
-                w = c_vecs[k, 0, 1]
-                answer[1, k, q] = answer[1, k, q] + (w if q == CUT - 1 else mv(c_maps[k, q + 1 - MID, 1], w))
-            if q == MID - 1:
-                for kk, qq in b_sent:
-                    if qq < MID:
-                        b_copy(kk, qq).start()
-        for k, q in b_sent:
-            if q >= MID:
-                b_copy(k, q).start()
-        for k, q in a_sent:
-            if MID <= q < CUT:
-                a_copy(k, q).start()
-
-        @pl.when(base == 0)
-        def _():
-            for k in range(2):
+            w = c_vecs[k, 0, 1]
+            for q in range(LEFT - 1, CUT):
+                answer[1, k, q] = answer[1, k, q] + (w if q == CUT - 1 else mv(c_maps[k, q + 1 - LEFT, 1], w))
+                if q == LEFT - 1:
+                    for j in range(LEFT):
+                        b_copy(k, j).start()
+                elif (k, q) != (1, MID):
+                    b_copy(k, q).start()
+            for q in range(LEFT, CUT):
+                if (k, q) != (1, MID):
+                    a_copy(k, q).start()
+
+            @pl.when(base == 0)
+            def _():
                 a_copy(k, CUT).start()
 
-        in_a[...] = answer[0, 1, MID]
-        in_b[...] = answer[1, 1, MID]
-
-    @pl.when(jnp.logical_not(is_mid) & (st != 0))
+            if k == 1:
+                in_a[...] = answer[0, 1, MID]
+                in_b[...] = answer[1, 1, MID]
+
+    @pl.when(jnp.logical_not(is_mid | is_sub) & (st != 0))
     def _():
         a_copy(0, 1).wait_recv()
 
@@ -419,13 +473,17 @@
 
     @pl.when(left & (pos > 0))
     def _():
+        @pl.when(unheard)
+        def _():
+            side_b_copy(0).start()
+
         y_out[...] = mv(maps[2], a_in) + vecs[1]
-        for q in range(MID - 1):
+        for q in range(LEFT - 1):
             @pl.when(pos > q)
             def _():
                 side_y_copy(q).start()
 
-    for e in range(1, MID):
+    for e in range(1, LEFT):
         @pl.when(pos < e)
         def _():
             pltpu.make_async_copy(maps.at[1], side_b.at[e], sbr_sem.at[e]).wait()
@@ -435,7 +493,7 @@
     def _():
         b_copy(0, 0).wait_recv()
 
-    for e in range(MID - 1, 0, -1):
+    for e in range(LEFT - 1, 0, -1):
         @pl.when(pos < e)
         def _():
             in_b[...] = mv(side_b[e], in_b[...]) + side_y[e]
@@ -454,9 +512,17 @@
             flow_v[:, pl.ds(i, 8, stride=8), :] + c_v[i] + mv(p_v[i], a_h) + mv(q_v[i], b_h)
         )
 
-    @pl.when(((pos > 0) & left) | near)
+    @pl.when(((pos > 0) & left & jnp.logical_not(is_sub)) | near)
     def _():
         map_copy(0).wait_send()
+
+    @pl.when(is_sub)
+    def _():
+        for k in range(2):
+            hop_copy(k).wait_send()
+            for q in range(1, SUB + 2):
+                if (k, q) != (1, SUB):
+                    a_copy(k, q).wait_send()
 
     @pl.when(near)
     def _():
@@ -467,11 +533,11 @@
         map_copy(2).wait_send()
         w_copy(centre, pos).wait_send()
 
-    @pl.when(jnp.logical_not(is_mid))
+    @pl.when(jnp.logical_not(is_mid | is_sub))
     def _():
         v_copy().wait_send()
 
-    for q in range(MID - 1):
+    for q in range(LEFT - 1):
         @pl.when(left & (pos > q))
         def _():
             side_b_copy(q).wait_send()
@@ -480,8 +546,14 @@
     @pl.when(is_mid)
     def _():
         for k, q in a_sent:
-            if q < CUT:
+            if LEFT <= q < CUT:
                 a_copy(k, q).wait_send()
+
+        @pl.when(base != 0)
+        def _():
+            for k, q in a_sent:
+                if q < LEFT:
+                    a_copy(k, q).wait_send()
 
         @pl.when(base == 0)
         def _():
@@ -524,10 +596,10 @@
             vm(5, 2, 8, 128), vm(5, 2, 8, 128), vm(ROW, 5, 4, 128), vm(5, 4, 128), vm(3, 5, 4, 128), vm(4, 5, 4, 128), vm(5, 4, 128),
             vm(3, 5, 5, 4, 128), vm(2, 5, 4, 128), vm(2, 5, 8, 128),
             vm(2, CUT, 3, 5, 5, 4, 128), vm(2, CUT, 2, 5, 4, 128), vm(2, 2, CUT + 1, 5, 4, 128),
-            vm(5, 4, 128), vm(5, 4, 128), vm(MID, 5, 5, 4, 128), vm(MID, 5, 4, 128), vm(5, 4, 128),
+            vm(5, 4, 128), vm(5, 4, 128), vm(LEFT, 5, 5, 4, 128), vm(LEFT, 5, 4, 128), vm(5, 4, 128), vm(2, 5, 4, 128),
             pltpu.SMEM((128,), jnp.int32), dma(7), dma(4), dma(4), dma(ROW), dma(ROW), dma(3), dma(3), pltpu.SemaphoreType.REGULAR,
-            dma(3), dma(2, CUT, 3), dma(2), dma(2, CUT, 2), dma(MID), dma(MID), dma(MID), dma(MID),
-            dma(2, CUT + 1), dma(1), dma(2, CUT + 1), dma(1),
+            dma(3), dma(2, CUT, 3), dma(2), dma(2, CUT, 2), dma(LEFT), dma(LEFT), dma(LEFT), dma(LEFT),
+            dma(2, CUT + 1), dma(1), dma(2, CUT + 1), dma(1), dma(2), dma(2),
         ],
         compiler_params=pltpu.CompilerParams(
             collective_id=0, has_side_effects=True, vmem_limit_bytes=60 * 1024 * 1024

time: 31.5 us -> 29.8 us (0.946)
  the two profiles are of different devices: /device:TPU:1 before, /device:TPU:262 now
where the time goes in v4:
time: 29.8 us; the launch traced here: 29.6 us
  Pallas kernels  28 us (94%)
  local copies, waits for them, and re-layouts  1.59 us (5%)
    pallas_call x1, Pallas kernels, local(): pl.pallas_call(kernel, out_shape=jax.ShapeDtypeStruct((NC, 64, 128), f32)...  28 us
    unnamed x1, local copies, waits for them, and re-layouts  1.59 us

profile of v4, /device:TPU:262, one launch (start us, length us, event | category | flops | bytes accessed | tf_op | source)
XLA Modules:
  0.0 29.6 jit_solution(10852037496654017047)
XLA Ops:
  0.0 28.0 %lusgs.1 = f32[5,64,128]{2,1,0:T(8,128)} custom-call(f32[5,64,128]{2,1,0:T(8,128)} %bitcast.39, f32[5,64,128]{2,1,0:T(8,128)} %bitcast.40, f32[64,128]{1,0:T(8,128)} %bitcast.41, f32[25,64,128]{2,1,0:T(8,128)} %bitcast.35, f32[25,64,128]{2,1,0:T(8,128)} %bitcast.36, f32[25,64,128]{2,1,0:T(8,128)} %bitcast.37, s32[128]{0:T(128)} %partner.1), custom_call_target="tpu_custom_call" | custom-call | tf_op jit(solution)/shard_map/lusgs/pallas_call | solution.py:588
  28.0 1.6 %copy.9 = f32[5,16,512]{2,1,0:T(8,128)} copy(f32[5,16,512]{2,1,0:T(8,128)} %bitcast.38) | data formatting | bytes 327680

commit v5 on v4

--- a/solution.py
+++ b/solution.py
@@ -26,13 +26,14 @@
 
 def kernel(
     flow, res, spr, dinv, low, upp, partner, out,
-    flow_v, res_v, spr_v, d_v, l_v, u_v, src_v,
+    out_0, out_1, out_2, out_3, out_4, out_sem, flow_v, res_v, spr_v, d_v, l_v, u_v, src_v,
     s_v, t_v, f_v, q_v, p_v, c_v,
     halo_lo, halo_hi, rot, rots, chosen, facing, ghost,
     maps, vecs, vh, c_maps, c_vecs, answer, in_a, in_b, side_b, side_y, y_out, hop_in,
-    part_s, ld_sem, hs_sem, hr_sem, gs_sem, gr_sem, xs_sem, xr_sem, ready,
+    part_s, ld_sem, hs_sem, hr_sem, gs_sem, gr_sem, xs_sem, xr_sem, ready, here,
     ms_sem, cm_sem, vs_sem, cv_sem, sbs_sem, sbr_sem, sys_sem, syr_sem, as_sem, ar_sem, bs_sem, br_sem, hs2_sem, hr2_sem,
 ):
+    outs = (out_0, out_1, out_2, out_3, out_4)
     st = lax.axis_index("stream")
     pt = lax.axis_index("pitch")
     up_p, dn_p = lax.rem(pt + 1, NPI), lax.rem(pt + NPI - 1, NPI)
@@ -45,8 +46,8 @@
     before = lax.rem(st + NS - CUT + MID, NS)
     is_mid = (pos == MID) & (core == 1)
     left = pos < LEFT
-    chained = (base == 0) & (pos <= SUB)
-    is_sub = (base == 0) & (pos == SUB) & (core == 1)
+    chained = pos <= SUB
+    is_sub = (pos == SUB) & (core == 1)
     home = jnp.where(chained, base + SUB, centre)
     unheard = (base == 0) & (pt == 0)
     near = (pos >= LEFT) & jnp.logical_not(is_mid)
@@ -71,7 +72,7 @@
 
     @pl.when(left)
     def _():
-        @pl.when((base != 0) | (pos >= SUB))
+        @pl.when(pos >= SUB)
         def _():
             pl.semaphore_signal(barrier, inc=1, **to(centre, pair + 1))
 
@@ -80,7 +81,7 @@
             def _():
                 pl.semaphore_signal(barrier, inc=1, **to(base + q, pt))
 
-    @pl.when((base == 0) & (pos == LEFT - 1))
+    @pl.when(pos == LEFT - 1)
     def _():
         pl.semaphore_signal(barrier, inc=1, **to(base + SUB, pair + 1))
 
@@ -106,13 +107,15 @@
     @pl.when(is_cut)
     def _():
         for nb in row_peers + column_peers:
-            pl.semaphore_signal(barrier, inc=1, **to(st, nb))
+            @pl.when(nb > pt)
+            def _():
+                pl.semaphore_signal(barrier, inc=1, **to(st, nb))
 
     for c in loads[1:]:
         c.start()
 
     expected = (
-        2 + jnp.where(is_cut, len(row_peers) + len(column_peers) + 1, 0) + jnp.where(is_mid, jnp.where(base == 0, 2 * (LEFT - SUB), 2 * LEFT), 0)
+        2 + jnp.where(is_cut, pt - row * ROW + row + 1, 0) + jnp.where(is_mid, 2 * (LEFT - SUB), 0)
         + jnp.where(near | (chained & jnp.logical_not(is_sub)), 1, 0) + jnp.where(is_sub, 2, 0)
         + jnp.where(left & (pos > 0), pos - jnp.where(unheard, 1, 0), 0)
     )
@@ -120,11 +123,15 @@
 
     @pl.when(is_mid)
     def _():
-        for q in range(LEFT):
-            for k in range(2):
-                @pl.when((base != 0) | (q == LEFT - 1) | ((q == SUB) & (k == 1)))
-                def _():
-                    pl.semaphore_signal(ready, inc=1, **to(base + q, pair + k))
+        for q, k in ((LEFT - 1, 0), (LEFT - 1, 1), (SUB, 1)):
+            pl.semaphore_signal(ready, inc=1, **to(base + q, pair + k))
+
+    @pl.when(is_cut)
+    def _():
+        for nb in row_peers + column_peers:
+            @pl.when(nb < pt)
+            def _():
+                pl.semaphore_signal(here, inc=1, **to(st, nb))
 
     loads[0].wait()
 
@@ -169,14 +176,6 @@
             who = part_s[nb * 4 + k]
             target[:, k : k + 1, :] = rot[lax.rem(who // 4, ROW), :, pl.ds(lax.rem(who, 4), 1), :]
 
-    @pl.when(is_cut)
-    def _():
-        rots[...] = flow_v[:, pl.ds(7, 4, stride=8), :]
-        rot[lax.rem(pt, ROW)] = flow_v[:, pl.ds(7, 4, stride=8), :]
-        pltpu.make_async_copy(partner, part_s, ld_sem.at[6]).start()
-        for c in row_copies():
-            c.start()
-
     for c in loads[1:4]:
         c.wait()
 
@@ -195,6 +194,20 @@
     keep = jnp.where(is_cut, 0.0, 1.0)
     m0, m1 = f_v[7, :, :, 0:4, :], f_v[7, :, :, 4:8, :]
     maps[0] = mm(m1, m0)
+
+    @pl.when(is_cut)
+    def _():
+        rots[...] = flow_v[:, pl.ds(7, 4, stride=8), :]
+        rot[lax.rem(pt, ROW)] = flow_v[:, pl.ds(7, 4, stride=8), :]
+        pltpu.make_async_copy(partner, part_s, ld_sem.at[6]).start()
+        higher = len(row_peers) + len(column_peers) - (pt - row * ROW) - row
+
+        @pl.when(higher > 0)
+        def _():
+            pl.semaphore_wait(here, higher)
+
+        for c in row_copies():
+            c.start()
 
     def map_copy(k, stream=home):
         slot = pos
@@ -329,7 +342,6 @@
             who = part_s[pt * 4 + k]
             ghost[:, k : k + 1, :] = facing[who // (4 * ROW), :, pl.ds(k, 1), :]
         vecs[0] = mv(m1, ghost[...]) + v1
-        pl.semaphore_wait(ready, 1)
         v_copy().start()
 
     def a_copy(k, q):
@@ -360,7 +372,7 @@
     def _():
         c_maps[1, SUB, 0] = maps[0]
         c_vecs[1, SUB, 0] = vecs[0]
-        for k in (1, 0):
+        def early(k):
             for q in range(SUB + 1):
                 if (k, q) != (1, SUB):
                     if q:
@@ -371,90 +383,160 @@
                 answer[0, k, q] = hop
                 if q <= SUB:
                     hop = mv(c_maps[k, q, 0], hop) + c_vecs[k, q, 0]
+
+        def tell(k):
+            hop_copy(k).start()
             for q in range(SUB + 1, 0, -1):
                 if (k, q) != (1, SUB):
                     a_copy(k, q).start()
             if k == 1:
                 in_a[...] = answer[0, 1, SUB]
-                pl.semaphore_wait(ready, 1)
-            hop_copy(k).start()
+
+        @pl.when(base == 0)
+        def _():
+            early(1)
+            for q in range(SUB + 1, 0, -1):
+                if q != SUB:
+                    a_copy(1, q).start()
+            in_a[...] = answer[0, 1, SUB]
+            pl.semaphore_wait(ready, 1)
+            hop_copy(1).start()
+            early(0)
+            tell(0)
+
+        @pl.when(base != 0)
+        def _():
+            pl.semaphore_wait(ready, 1)
+            early(0)
+            early(1)
+            tell(0)
+            tell(1)
+
+    def arrived_right(k):
+        arrived_map(k, LEFT - 1, 0)
+        arrived_vec(k, LEFT - 1, 0)
+        for q in range(LEFT, CUT):
+            if (k, q) != (1, MID):
+                for m in range(3):
+                    arrived_map(k, q, m)
+                for m in range(2):
+                    arrived_vec(k, q, m)
+        for q in range(CUT - 2, LEFT - 1, -1):
+            c_maps[k, q - LEFT, 1] = mm(c_maps[k, q, 1], c_maps[k, q + 1, 1] if q == CUT - 2 else c_maps[k, q + 1 - LEFT, 1])
+
+        @pl.when(base == 0)
+        def _():
+            arrived_map(k, 0, 2)
+
+        @pl.when(base != 0)
+        def _():
+            c_maps[k, 0, 2] = jnp.zeros((NC, NC, 4, 128), jnp.float32)
+            c_vecs[k, 0, 1] = jnp.zeros((NC, 4, 128), jnp.float32)
+
+    def right_values(k, a, stop):
+        for q in range(LEFT, CUT):
+            answer[0, k, q] = a
+            a = mv(c_maps[k, q, 0], a) + c_vecs[k, q, 0]
+        answer[0, k, CUT] = a
+        b = mv(c_maps[k, 0, 2], a)
+        answer[1, k, CUT - 1] = b
+        for q in range(CUT - 1, stop, -1):
+            b = mv(c_maps[k, q, 1], b) + mv(c_maps[k, q, 2], answer[0, k, q]) + c_vecs[k, q, 1]
+            answer[1, k, q - 1] = b
+
+    def heard(k):
+        hop_copy(k).wait_recv()
+        answer[0, k, LEFT - 1] = hop_in[k]
+        return mv(c_maps[k, LEFT - 1, 0], hop_in[k]) + c_vecs[k, LEFT - 1, 0]
+
+    def solve(k):
+        arrived_right(k)
+        a = heard(k)
+        right_values(k, a, LEFT - 1)
+
+    def prepare(k):
+        arrived_right(k)
+        back = c_maps[k, 0, 2]
+        for q in range(CUT - 1, LEFT - 1, -1):
+            back = c_maps[k, q, 2] + mm(c_maps[k, q, 1], mm(back, c_maps[k, q, 0]))
+        c_maps[k, LEFT - 2, 1] = mm(back, c_maps[k, LEFT - 1, 0])
+        right_values(k, c_vecs[k, LEFT - 1, 0], LEFT - 1)
+
+    def finish(k, late):
+        if late:
+            hop_copy(k).wait_recv()
+            answer[1, k, LEFT - 1] = answer[1, k, LEFT - 1] + mv(c_maps[k, LEFT - 2, 1], hop_in[k])
+
+        @pl.when(base == 0)
+        def _():
+            arrived_vec(k, 0, 1)
+
+        w = c_vecs[k, 0, 1]
+        answer[1, k, LEFT - 1] = answer[1, k, LEFT - 1] + mv(c_maps[k, 0, 1], w)
+        b_copy(k, 0).start()
+
+    def finish_left(cores):
+        for j in range(1, LEFT):
+            for k in cores:
+                b_copy(k, j).start()
+
+    def finish_right(k, late):
+        if late:
+            right_values(k, mv(c_maps[k, LEFT - 1, 0], hop_in[k]) + c_vecs[k, LEFT - 1, 0], LEFT)
+        w = c_vecs[k, 0, 1]
+        for q in range(LEFT, CUT):
+            if q == CUT - 1:
+                more = w
+            else:
+                more = mv(c_maps[k, CUT - 1, 1] if q == CUT - 2 else c_maps[k, q + 1 - LEFT, 1], w)
+            answer[1, k, q] = answer[1, k, q] + more
+            if (k, q) != (1, MID):
+                b_copy(k, q).start()
+                a_copy(k, q).start()
+
+        @pl.when(base == 0)
+        def _():
+            a_copy(k, CUT).start()
+
+        if k == 1:
+            in_a[...] = answer[0, 1, MID]
+            in_b[...] = answer[1, 1, MID]
 
     @pl.when(is_mid)
     def _():
         c_maps[1, MID] = maps[...]
         c_vecs[1, MID] = vecs[...]
-        for k in (1, 0):
-            @pl.when(base == 0)
-            def _():
-                hop_copy(k).wait_recv()
-                answer[0, k, LEFT - 1] = hop_in[k]
-
-            @pl.when(base != 0)
-            def _():
-                for q in range(LEFT - 1):
-                    if q:
-                        arrived_map(k, q, 0)
-                    arrived_vec(k, q, 0)
-                early = c_vecs[k, 0, 0]
-                for q in range(1, LEFT):
-                    answer[0, k, q] = early
-                    a_copy(k, q).start()
-                    if q < LEFT - 1:
-                        early = mv(c_maps[k, q, 0], early) + c_vecs[k, q, 0]
-
-            arrived_map(k, LEFT - 1, 0)
-            arrived_vec(k, LEFT - 1, 0)
-            a = mv(c_maps[k, LEFT - 1, 0], answer[0, k, LEFT - 1]) + c_vecs[k, LEFT - 1, 0]
-            answer[0, k, LEFT] = a
-            for q in range(LEFT, CUT):
-                if (k, q) != (1, MID):
-                    for m in range(3):
-                        arrived_map(k, q, m)
-                    for m in range(2):
-                        arrived_vec(k, q, m)
-
-            @pl.when(base == 0)
-            def _():
-                arrived_map(k, 0, 2)
-
-            @pl.when(base != 0)
-            def _():
-                c_maps[k, 0, 2] = jnp.zeros((NC, NC, 4, 128), jnp.float32)
-                c_vecs[k, 0, 1] = jnp.zeros((NC, 4, 128), jnp.float32)
-
-            for q in range(LEFT, CUT):
-                a = mv(c_maps[k, q, 0], a) + c_vecs[k, q, 0]
-                answer[0, k, q + 1] = a
-            b = mv(c_maps[k, 0, 2], a)
-            answer[1, k, CUT - 1] = b
-            for q in range(CUT - 1, LEFT - 1, -1):
-                b = mv(c_maps[k, q, 1], b) + mv(c_maps[k, q, 2], answer[0, k, q]) + c_vecs[k, q, 1]
-                answer[1, k, q - 1] = b
-                c_maps[k, q - LEFT, 1] = c_maps[k, q, 1] if q == CUT - 1 else mm(c_maps[k, q, 1], c_maps[k, q + 1 - LEFT, 1])
-
-            @pl.when(base == 0)
-            def _():
-                arrived_vec(k, 0, 1)
-
-            w = c_vecs[k, 0, 1]
-            for q in range(LEFT - 1, CUT):
-                answer[1, k, q] = answer[1, k, q] + (w if q == CUT - 1 else mv(c_maps[k, q + 1 - LEFT, 1], w))
-                if q == LEFT - 1:
-                    for j in range(LEFT):
-                        b_copy(k, j).start()
-                elif (k, q) != (1, MID):
-                    b_copy(k, q).start()
-            for q in range(LEFT, CUT):
-                if (k, q) != (1, MID):
-                    a_copy(k, q).start()
-
-            @pl.when(base == 0)
-            def _():
-                a_copy(k, CUT).start()
-
-            if k == 1:
-                in_a[...] = answer[0, 1, MID]
-                in_b[...] = answer[1, 1, MID]
+
+        @pl.when(base != 0)
+        def _():
+            prepare(1)
+            prepare(0)
+            finish(0, True)
+            finish(1, True)
+            finish_left((0, 1))
+            finish_right(0, True)
+            finish_right(1, True)
+
+        @pl.when((base == 0) & (pair == 0))
+        def _():
+            solve(1)
+            finish(1, False)
+            finish_left((1,))
+            prepare(0)
+            finish(0, True)
+            finish_left((0,))
+            finish_right(1, False)
+            finish_right(0, True)
+
+        @pl.when((base == 0) & (pair != 0))
+        def _():
+            solve(1)
+            solve(0)
+            finish(0, False)
+            finish(1, False)
+            finish_left((0, 1))
+            finish_right(0, False)
+            finish_right(1, False)
 
     @pl.when(jnp.logical_not(is_mid | is_sub) & (st != 0))
     def _():
@@ -483,34 +565,54 @@
             def _():
                 side_y_copy(q).start()
 
+    a1 = jnp.where(is_cut, ghost[...], mv(m0, a_in) + v0)
+    vh[0, :, 0:4, :] = a_in
+    vh[0, :, 4:8, :] = a1
+    a_h = vh[0]
+    for i in range(8):
+        part = flow_v[:, pl.ds(i, 8, stride=8), :] + c_v[i] + mv(p_v[i], a_h)
+        for c in range(NC):
+            outs[c][pl.ds(i, 8, stride=8), :] = part[c]
+    half_b = mv(w1, a1) + ww1
+
     for e in range(1, LEFT):
         @pl.when(pos < e)
         def _():
             pltpu.make_async_copy(maps.at[1], side_b.at[e], sbr_sem.at[e]).wait()
             pltpu.make_async_copy(y_out, side_y.at[e], syr_sem.at[e]).wait()
 
+    for e in range(LEFT - 1, 1, -1):
+        @pl.when(pos < e - 1)
+        def _():
+            side_y[e - 1] = mv(side_b[e - 1], side_y[e]) + side_y[e - 1]
+            side_b[e - 1] = mm(side_b[e - 1], side_b[e])
+
     @pl.when(jnp.logical_not(is_mid))
     def _():
         b_copy(0, 0).wait_recv()
 
-    for e in range(LEFT - 1, 0, -1):
-        @pl.when(pos < e)
+    for e in range(1, LEFT):
+        @pl.when(pos == e - 1)
         def _():
             in_b[...] = mv(side_b[e], in_b[...]) + side_y[e]
 
     b_in = in_b[...] * jnp.where(st == NS - 1, 0.0, 1.0)
-
-    a1 = jnp.where(is_cut, ghost[...], mv(m0, a_in) + v0)
-    b_h0 = (mv(b1, b_in) + mv(w1, a1) + ww1) * keep
-    vh[0, :, 0:4, :] = a_in
-    vh[0, :, 4:8, :] = a1
-    vh[1, :, 0:4, :] = b_h0
+    vh[1, :, 0:4, :] = (mv(b1, b_in) + half_b) * keep
     vh[1, :, 4:8, :] = b_in
-    a_h, b_h = vh[0], vh[1]
-    for i in range(8):
-        out[:, pl.ds(i, 8, stride=8), :] = (
-            flow_v[:, pl.ds(i, 8, stride=8), :] + c_v[i] + mv(p_v[i], a_h) + mv(q_v[i], b_h)
-        )
+    b_h = vh[1]
+
+    def out_copy(c):
+        return pltpu.make_async_copy(outs[c], out.at[c], out_sem.at[c])
+
+    for c in range(NC):
+        for i in range(8):
+            outs[c][pl.ds(i, 8, stride=8), :] = outs[c][pl.ds(i, 8, stride=8), :] + sum(
+                q_v[i, c, k] * b_h[k] for k in range(NC)
+            )
+        out_copy(c).start()
+
+    for c in range(NC):
+        out_copy(c).wait()
 
     @pl.when(((pos > 0) & left & jnp.logical_not(is_sub)) | near)
     def _():
@@ -549,11 +651,6 @@
             if LEFT <= q < CUT:
                 a_copy(k, q).wait_send()
 
-        @pl.when(base != 0)
-        def _():
-            for k, q in a_sent:
-                if q < LEFT:
-                    a_copy(k, q).wait_send()
 
         @pl.when(base == 0)
         def _():
@@ -589,15 +686,16 @@
         kernel,
         out_shape=jax.ShapeDtypeStruct((NC, 64, 128), f32),
         in_specs=[hbm] * 7,
-        out_specs=pl.BlockSpec(memory_space=pltpu.VMEM),
+        out_specs=hbm,
         scratch_shapes=[
+            vm(64, 128), vm(64, 128), vm(64, 128), vm(64, 128), vm(64, 128), dma(NC),
             vm(5, 64, 128), vm(5, 64, 128), vm(64, 128), vm(25, 64, 128), vm(25, 64, 128), vm(25, 64, 128), vm(5, 64, 128),
             vm(8, 5, 5, 8, 128), vm(8, 5, 5, 8, 128), vm(8, 5, 5, 8, 128), vm(8, 5, 5, 8, 128), vm(8, 5, 5, 8, 128), vm(8, 5, 8, 128),
             vm(5, 2, 8, 128), vm(5, 2, 8, 128), vm(ROW, 5, 4, 128), vm(5, 4, 128), vm(3, 5, 4, 128), vm(4, 5, 4, 128), vm(5, 4, 128),
             vm(3, 5, 5, 4, 128), vm(2, 5, 4, 128), vm(2, 5, 8, 128),
             vm(2, CUT, 3, 5, 5, 4, 128), vm(2, CUT, 2, 5, 4, 128), vm(2, 2, CUT + 1, 5, 4, 128),
             vm(5, 4, 128), vm(5, 4, 128), vm(LEFT, 5, 5, 4, 128), vm(LEFT, 5, 4, 128), vm(5, 4, 128), vm(2, 5, 4, 128),
-            pltpu.SMEM((128,), jnp.int32), dma(7), dma(4), dma(4), dma(ROW), dma(ROW), dma(3), dma(3), pltpu.SemaphoreType.REGULAR,
+            pltpu.SMEM((128,), jnp.int32), dma(7), dma(4), dma(4), dma(ROW), dma(ROW), dma(3), dma(3), pltpu.SemaphoreType.REGULAR, pltpu.SemaphoreType.REGULAR,
             dma(3), dma(2, CUT, 3), dma(2), dma(2, CUT, 2), dma(LEFT), dma(LEFT), dma(LEFT), dma(LEFT),
             dma(2, CUT + 1), dma(1), dma(2, CUT + 1), dma(1), dma(2), dma(2),
         ],

time: 29.8 us -> 29.4 us (0.987)
  the two profiles are of different devices: /device:TPU:262 before, /device:TPU:257 now
where the time goes in v5:
time: 29.4 us; the launch traced here: 29.3 us
  Pallas kernels  27.7 us (94%)
  local copies, waits for them, and re-layouts  1.59 us (5%)
    pallas_call x1, Pallas kernels, local(): pl.pallas_call(kernel, out_shape=jax.ShapeDtypeStruct((NC, 64, 128), f32)...  27.7 us
    unnamed x1, local copies, waits for them, and re-layouts  1.59 us

profile of v5, /device:TPU:257, one launch (start us, length us, event | category | flops | bytes accessed | tf_op | source)
XLA Modules:
  0.0 29.3 jit_solution(15408295719999637509)
XLA Ops:
  0.0 27.7 %lusgs.1 = f32[5,64,128]{2,1,0:T(8,128)} custom-call(f32[5,64,128]{2,1,0:T(8,128)} %bitcast.39, f32[5,64,128]{2,1,0:T(8,128)} %bitcast.40, f32[64,128]{1,0:T(8,128)} %bitcast.41, f32[25,64,128]{2,1,0:T(8,128)} %bitcast.35, f32[25,64,128]{2,1,0:T(8,128)} %bitcast.36, f32[25,64,128]{2,1,0:T(8,128)} %bitcast.37, s32[128]{0:T(128)} %partner.1), custom_call_target="tpu_custom_call" | custom-call | tf_op jit(solution)/shard_map/lusgs/pallas_call | solution.py:685
  27.7 1.6 %copy.9 = f32[5,16,512]{2,1,0:T(8,128)} copy(f32[5,16,512]{2,1,0:T(8,128)} %bitcast.38) | data formatting | bytes 327680

commit v6 on v5

--- a/solution.py
+++ b/solution.py
@@ -42,9 +42,17 @@
     base = st - pos
     core = lax.rem(pt, 2)
     pair = pt - core
-    centre = base + MID
+    mid = jnp.where(base == 0, MID, MID - 1)
+    centre = base + mid
     before = lax.rem(st + NS - CUT + MID, NS)
-    is_mid = (pos == MID) & (core == 1)
+    is_mid = (pos == mid) & (core == 1)
+
+    def unless_mid(k, q, act):
+        if k == 0 or q not in (MID - 1, MID):
+            act()
+        else:
+            pl.when(mid != q)(act)
+
     left = pos < LEFT
     chained = pos <= SUB
     is_sub = (pos == SUB) & (core == 1)
@@ -96,8 +104,10 @@
     def _():
         for q in range(LEFT, CUT):
             for k in range(2):
-                if (q, k) != (MID, 1):
+                def greet(q=q, k=k):
                     pl.semaphore_signal(barrier, inc=1, **to(base + q, pair + k))
+
+                unless_mid(k, q, greet)
 
         @pl.when(base == 0)
         def _():
@@ -262,11 +272,11 @@
     for h in range(2):
         for c in range(4):
             r = h * 32 + c * 8
-            mid = flow_v[:, r : r + 8, :]
+            here_v = flow_v[:, r : r + 8, :]
             lo = halo_lo[:, h] if c == 0 else flow_v[:, r - 8 : r, :]
             hi = halo_hi[:, h] if c == 3 else flow_v[:, r + 8 : r + 16, :]
             src_v[:, r : r + 8, :] = res_v[:, r : r + 8, :] + spr_v[r : r + 8, :][None] * (
-                hi + lo - 2.0 * mid
+                hi + lo - 2.0 * here_v
             )
 
     star = None
@@ -365,8 +375,8 @@
             answer.at[0, k, SUB + 1], hop_in.at[k], hs2_sem.at[k], hr2_sem.at[k], **to(centre, pt)
         )
 
-    a_sent = [(k, q) for q in range(1, CUT + 1) for k in range(2) if (k, q) != (1, MID)]
-    b_sent = [(k, q) for q in range(CUT) for k in range(2) if (k, q) != (1, MID)]
+    a_sent = [(k, q) for q in range(1, CUT + 1) for k in range(2)]
+    b_sent = [(k, q) for q in range(CUT) for k in range(2)]
 
     @pl.when(is_sub)
     def _():
@@ -416,11 +426,13 @@
         arrived_map(k, LEFT - 1, 0)
         arrived_vec(k, LEFT - 1, 0)
         for q in range(LEFT, CUT):
-            if (k, q) != (1, MID):
+            def arrived(q=q):
                 for m in range(3):
                     arrived_map(k, q, m)
                 for m in range(2):
                     arrived_vec(k, q, m)
+
+            unless_mid(k, q, arrived)
         for q in range(CUT - 2, LEFT - 1, -1):
             c_maps[k, q - LEFT, 1] = mm(c_maps[k, q, 1], c_maps[k, q + 1, 1] if q == CUT - 2 else c_maps[k, q + 1 - LEFT, 1])
 
@@ -490,22 +502,25 @@
             else:
                 more = mv(c_maps[k, CUT - 1, 1] if q == CUT - 2 else c_maps[k, q + 1 - LEFT, 1], w)
             answer[1, k, q] = answer[1, k, q] + more
-            if (k, q) != (1, MID):
+
+            def answers(q=q):
                 b_copy(k, q).start()
                 a_copy(k, q).start()
 
+            unless_mid(k, q, answers)
+
         @pl.when(base == 0)
         def _():
             a_copy(k, CUT).start()
 
         if k == 1:
-            in_a[...] = answer[0, 1, MID]
-            in_b[...] = answer[1, 1, MID]
+            in_a[...] = answer[0, 1, mid]
+            in_b[...] = answer[1, 1, mid]
 
     @pl.when(is_mid)
     def _():
-        c_maps[1, MID] = maps[...]
-        c_vecs[1, MID] = vecs[...]
+        c_maps[1, mid] = maps[...]
+        c_vecs[1, mid] = vecs[...]
 
         @pl.when(base != 0)
         def _():
@@ -649,7 +664,7 @@
     def _():
         for k, q in a_sent:
             if LEFT <= q < CUT:
-                a_copy(k, q).wait_send()
+                unless_mid(k, q, lambda k=k, q=q: a_copy(k, q).wait_send())
 
 
         @pl.when(base == 0)
@@ -658,7 +673,7 @@
                 a_copy(k, CUT).wait_send()
 
         for k, q in b_sent:
-            b_copy(k, q).wait_send()
+            unless_mid(k, q, lambda k=k, q=q: b_copy(k, q).wait_send())
 
 
 def to_tiles(x):

time: 29.4 us -> 29 us (0.986)
  the two profiles are of different devices: /device:TPU:257 before, /device:TPU:32 now
where the time goes in v6:
time: 29 us; the launch traced here: 28.9 us
  Pallas kernels  27.3 us (94%)
  local copies, waits for them, and re-layouts  1.59 us (5%)
    pallas_call x1, Pallas kernels, local(): pl.pallas_call(kernel, out_shape=jax.ShapeDtypeStruct((NC, 64, 128), f32)...  27.3 us
    unnamed x1, local copies, waits for them, and re-layouts  1.59 us

profile of v6, /device:TPU:32, one launch (start us, length us, event | category | flops | bytes accessed | tf_op | source)
XLA Modules:
  0.0 28.9 jit_solution(8805373389134881398)
XLA Ops:
  0.0 27.3 %lusgs.1 = f32[5,64,128]{2,1,0:T(8,128)} custom-call(f32[5,64,128]{2,1,0:T(8,128)} %bitcast.39, f32[5,64,128]{2,1,0:T(8,128)} %bitcast.40, f32[64,128]{1,0:T(8,128)} %bitcast.41, f32[25,64,128]{2,1,0:T(8,128)} %bitcast.35, f32[25,64,128]{2,1,0:T(8,128)} %bitcast.36, f32[25,64,128]{2,1,0:T(8,128)} %bitcast.37, s32[128]{0:T(128)} %partner.1), custom_call_target="tpu_custom_call" | custom-call | tf_op jit(solution)/shard_map/lusgs/pallas_call | solution.py:700
  27.3 1.6 %copy.9 = f32[5,16,512]{2,1,0:T(8,128)} copy(f32[5,16,512]{2,1,0:T(8,128)} %bitcast.38) | data formatting | bytes 327680

commit v7 on v6

--- a/solution.py
+++ b/solution.py
@@ -536,10 +536,9 @@
         def _():
             solve(1)
             finish(1, False)
-            finish_left((1,))
             prepare(0)
             finish(0, True)
-            finish_left((0,))
+            finish_left((0, 1))
             finish_right(1, False)
             finish_right(0, True)
 

time: 29 us -> 29.3 us (1.010); the launches traced: 28.9 us -> 28.9 us
  no operation moved by 1% of the time
where the time goes in v7:
time: 29.3 us; the launch traced here: 28.9 us
  Pallas kernels  27.3 us (93%)
  local copies, waits for them, and re-layouts  1.59 us (5%)
    pallas_call x1, Pallas kernels, local(): pl.pallas_call(kernel, out_shape=jax.ShapeDtypeStruct((NC, 64, 128), f32)...  27.3 us
    unnamed x1, local copies, waits for them, and re-layouts  1.59 us

profile of v7, /device:TPU:32, one launch (start us, length us, event | category | flops | bytes accessed | tf_op | source)
XLA Modules:
  0.0 28.9 jit_solution(2032144137362741421)
XLA Ops:
  0.0 27.3 %lusgs.1 = f32[5,64,128]{2,1,0:T(8,128)} custom-call(f32[5,64,128]{2,1,0:T(8,128)} %bitcast.39, f32[5,64,128]{2,1,0:T(8,128)} %bitcast.40, f32[64,128]{1,0:T(8,128)} %bitcast.41, f32[25,64,128]{2,1,0:T(8,128)} %bitcast.35, f32[25,64,128]{2,1,0:T(8,128)} %bitcast.36, f32[25,64,128]{2,1,0:T(8,128)} %bitcast.37, s32[128]{0:T(128)} %partner.1), custom_call_target="tpu_custom_call" | custom-call | tf_op jit(solution)/shard_map/lusgs/pallas_call | solution.py:699
  27.3 1.6 %copy.9 = f32[5,16,512]{2,1,0:T(8,128)} copy(f32[5,16,512]{2,1,0:T(8,128)} %bitcast.38) | data formatting | bytes 327680
